TPU v7x, 32 devices: a whole 2x2x4 slice. The times are simulated.
32 devices in a mesh: batch: 8 (over y, x, core), seq: 4 (over z).
Axes of the slice: x: 2, y: 2, z: 4, core: 2. Of those that a mesh axis runs over, the one named last changes fastest.
Arguments:
- tokens: bfloat16 [8, 1024, 1024], P('batch', 'seq'), may hold values from -6 to 6
- norm_gain1: float32 [1024], replicated, may hold values from 0.1 to 1.9
- w_in: bfloat16 [1024, 3072], replicated, may hold values from -0.1875 to 0.1875
- short_kernel: bfloat16 [3, 3072], replicated, may hold values from -1 to 1
- filt_w1: float32 [33, 64], replicated, may hold values from -1.75 to 1.75
- filt_w2: float32 [64, 64], replicated, may hold values from -1 to 1
- filt_w3: float32 [64, 1024], replicated, may hold values from -0.046875 to 0.046875
- decay_rate: float32 [1024], replicated, may hold values from 0 to 1, as said below
- conv_bias: float32 [1024], replicated, may hold values from -4 to 4
- w_out: bfloat16 [1024, 1024], replicated, may hold values from -0.1875 to 0.1875
- norm_gain2: float32 [1024], replicated, may hold values from 0.1 to 1.9
- w_up: bfloat16 [1024, 4096], replicated, may hold values from -0.1875 to 0.1875
- w_down: bfloat16 [4096, 1024], replicated, may hold values from -0.09375 to 0.09375
- cotangent: bfloat16 [8, 1024, 1024], P('batch', 'seq'), may hold values from -6 to 6
Outputs:
- layer_out: bfloat16 [8, 1024, 1024], P('batch', 'seq')
- tokens_grad: float32 [8, 1024, 1024], P('batch', 'seq')
- grad_gain1: float32 [1024], P(('batch', 'seq'))
- grad_w_in: float32 [1024, 3072], P(('batch', 'seq'))
- grad_short: float32 [3, 3072], P(None, ('batch', 'seq'))
- grad_filt_w1: float32 [33, 64], replicated
- grad_filt_w2: float32 [64, 64], replicated
- grad_filt_w3: float32 [64, 1024], P(None, ('batch', 'seq'))
- grad_conv_bias: float32 [1024], P(('batch', 'seq'))
- grad_w_out: float32 [1024, 1024], P(('batch', 'seq'))
- grad_gain2: float32 [1024], P(('batch', 'seq'))
- grad_w_up: float32 [1024, 4096], P(('batch', 'seq'))
- grad_w_down: float32 [4096, 1024], P(('batch', 'seq'))
Inputs may be any that keep to these rules, and one draw needn't show every extreme that they name: `decay_rate`: positive per-lag decay rates.
All inputs are finite; a program needn't handle non-finite values.
Results may differ from a plain program's by a relative error of at most 0.012.
Values may be sent and summed in bfloat16 or wider, within the bound.
A program may use at most 256 MiB of HBM per device.

v0:
```python
import functools
import math

import jax
import jax.numpy as jnp
from jax import lax
from jax.sharding import PartitionSpec as P


def from_behind(value, axis, steps):
    count = lax.axis_size(axis)
    first, last = (max(0, -steps), min(count, count - steps))
    return lax.ppermute(value, axis, [(source, source + steps) for source in range(first, last)])


def layer_norm(values, gain):
    average = jnp.mean(values, axis=-1, keepdims=True)
    centered = values - average
    spread_sq = jnp.mean(centered * centered, axis=-1, keepdims=True)
    return centered * lax.rsqrt(spread_sq + 1e-05) * gain


def smooth_gelu(values):
    return jax.nn.gelu(values, approximate=True)


def filter_taps(w_first, w_second, w_third, decay_rate, seq_len):
    band_count = (w_first.shape[0] - 1) // 2
    lag_index = jnp.arange(seq_len).astype(jnp.float32)
    lag_scaled = lag_index / (seq_len - 1)
    lag_angle = lag_index * (2.0 * math.pi / seq_len)
    band_freq = 0.0001 + jnp.arange(band_count).astype(jnp.float32) * (
        (band_count - 1 - 0.0001) / (band_count - 1)
    )
    phases = lag_angle[:, None] * band_freq[None, :]
    features = jnp.concatenate([lag_scaled[:, None], jnp.cos(phases), -jnp.sin(phases)], axis=1)
    hidden_one = jnp.sin(
        jnp.dot(
            features, w_first, precision=lax.Precision.HIGHEST, preferred_element_type=jnp.float32
        )
    )
    hidden_two = jnp.sin(
        jnp.dot(
            hidden_one,
            w_second,
            precision=lax.Precision.HIGHEST,
            preferred_element_type=jnp.float32,
        )
    )
    filt_raw = jnp.dot(
        hidden_two, w_third, precision=lax.Precision.HIGHEST, preferred_element_type=jnp.float32
    )
    return filt_raw * jnp.exp(-decay_rate[None, :] * lag_index[:, None])


def dft_tables(block_len):
    span_len = 2 * block_len
    indices = jnp.arange(span_len, dtype=jnp.int32)
    products = indices[:, None] * indices[None, :] % span_len
    angles = products.astype(jnp.float32) * (2.0 * math.pi / span_len)
    cosine = jnp.cos(angles)
    sines = jnp.sin(angles)
    forward_table = jnp.concatenate([cosine, -sines], axis=0)
    inverse_table = jnp.concatenate([cosine, -sines], axis=1) / span_len
    return (forward_table, inverse_table)


def split_table(table):
    upper = table.astype(jnp.bfloat16)
    lower = (table - upper.astype(jnp.float32)).astype(jnp.bfloat16)
    return (upper, lower)


def transform(pair, block):
    first = jnp.einsum("fn,snd->sfd", pair[0], block, preferred_element_type=jnp.float32)
    return first + jnp.einsum("fn,snd->sfd", pair[1], block, preferred_element_type=jnp.float32)


def spec_mul(first_spec, second_spec):
    left_re, left_im = jnp.split(first_spec, 2, axis=-2)
    right_re, right_im = jnp.split(second_spec, 2, axis=-2)
    return jnp.concatenate(
        [left_re * right_re - left_im * right_im, left_re * right_im + left_im * right_re], axis=-2
    )


def spec_conj_mul(first_spec, second_spec):
    left_re, left_im = jnp.split(first_spec, 2, axis=-2)
    right_re, right_im = jnp.split(second_spec, 2, axis=-2)
    return jnp.concatenate(
        [left_re * right_re + left_im * right_im, left_re * right_im - left_im * right_re], axis=-2
    )


def on_device(
    tokens,
    norm_gain1,
    w_in,
    short_kernel,
    filt_w1,
    filt_w2,
    filt_w3,
    decay_rate,
    conv_bias,
    w_out,
    norm_gain2,
    w_up,
    w_down,
    cotangent,
):
    highest = lax.Precision.HIGHEST
    num_seqs, block_len, features_count = tokens.shape
    span_len = 2 * block_len
    spec_len = 2 * span_len
    blocks = lax.axis_size("seq")
    position = lax.axis_index("seq")
    seq_len = block_len * blocks
    forward_table, inverse_table = dft_tables(block_len)
    full_pair = split_table(forward_table)
    head_pair = split_table(forward_table[:, :block_len])
    tail_pair = split_table(forward_table[:, block_len:])
    inputs = tokens.astype(jnp.float32)
    normed1, norm1_back = jax.vjp(layer_norm, inputs, norm_gain1)
    normed1 = normed1.astype(jnp.bfloat16)
    projected = jnp.einsum("std,de->ste", normed1, w_in, preferred_element_type=jnp.float32).astype(
        jnp.bfloat16
    )
    earlier = from_behind(projected[:, block_len - 2 :], "seq", 1)
    extended = jnp.concatenate([earlier, projected], axis=1).astype(jnp.float32)
    kernel = short_kernel.astype(jnp.float32)
    mixed = (
        kernel[0] * extended[:, 2:]
        + kernel[1] * extended[:, 1 : block_len + 1]
        + kernel[2] * extended[:, :block_len]
    )
    gate_out = mixed[..., :features_count]
    gate_in = mixed[..., features_count : 2 * features_count]
    values = mixed[..., 2 * features_count :]
    signal = (values * gate_in).astype(jnp.bfloat16)
    signal_wide = signal.astype(jnp.float32)
    filt_taps, filter_back = jax.vjp(
        functools.partial(filter_taps, decay_rate=decay_rate, seq_len=seq_len),
        filt_w1,
        filt_w2,
        filt_w3,
    )
    taps_low = filt_taps.astype(jnp.bfloat16)
    taps_blocks = taps_low.reshape(blocks, block_len, features_count)
    zero_taps = jnp.zeros((1, block_len, features_count), jnp.bfloat16)
    zero_block = jnp.zeros((1, block_len, features_count), jnp.float32)
    segments = jnp.concatenate(
        [jnp.concatenate([zero_taps, taps_blocks[:-1]], axis=0), taps_blocks], axis=1
    )
    filter_spec = transform(full_pair, segments)

    def filter_at(lag_steps):
        return lax.dynamic_index_in_dim(
            filter_spec, jnp.clip(lag_steps, 0, blocks - 1), 0, keepdims=False
        )

    zero_spec = jnp.zeros((num_seqs, spec_len, features_count), jnp.float32)
    running = zero_spec
    portion = lax.all_gather(signal, "seq", axis=1, tiled=True)
    offset = jnp.int32(0)
    for member in range(portion.shape[1] // block_len):
        block = portion[:, member * block_len : (member + 1) * block_len]
        accumulate_lag_steps = position - (offset // block_len + member)
        running = running + jnp.where(
            accumulate_lag_steps >= 0,
            spec_mul(filter_at(accumulate_lag_steps)[None], transform(head_pair, block)),
            0.0,
        )
    conv_out = jnp.einsum(
        "nf,sfd->snd",
        inverse_table[block_len:],
        running,
        precision=highest,
        preferred_element_type=jnp.float32,
    )
    long_out = conv_out + conv_bias * signal_wide
    gated = (long_out * gate_out).astype(jnp.bfloat16)
    residual1 = inputs + jnp.einsum("std,de->ste", gated, w_out, preferred_element_type=jnp.float32)
    normed2, norm2_back = jax.vjp(layer_norm, residual1, norm_gain2)
    normed2 = normed2.astype(jnp.bfloat16)
    hidden_pre = jnp.einsum("std,df->stf", normed2, w_up, preferred_element_type=jnp.float32)
    hidden_act, gelu_back = jax.vjp(smooth_gelu, hidden_pre)
    hidden = hidden_act.astype(jnp.bfloat16)
    result = residual1 + jnp.einsum(
        "stf,fd->std", hidden, w_down, preferred_element_type=jnp.float32
    )
    layer_out = result.astype(jnp.bfloat16)
    grad_down = jnp.einsum("stf,std->fd", hidden, cotangent, preferred_element_type=jnp.float32)
    grad_hidden = jnp.einsum("std,fd->stf", cotangent, w_down, preferred_element_type=jnp.float32)
    grad_pre = gelu_back(grad_hidden)[0].astype(jnp.bfloat16)
    grad_up = jnp.einsum("std,stf->df", normed2, grad_pre, preferred_element_type=jnp.float32)
    grad_norm2 = jnp.einsum("stf,df->std", grad_pre, w_up, preferred_element_type=jnp.float32)
    grad_res, grad_gain2 = norm2_back(grad_norm2)
    grad_res = grad_res + cotangent.astype(jnp.float32)
    grad_branch = grad_res.astype(jnp.bfloat16)
    grad_out_w = jnp.einsum("std,ste->de", gated, grad_branch, preferred_element_type=jnp.float32)
    grad_gated = jnp.einsum("ste,de->std", grad_branch, w_out, preferred_element_type=jnp.float32)
    grad_long = (grad_gated * gate_out).astype(jnp.bfloat16)
    grad_long_wide = grad_long.astype(jnp.float32)
    grad_gate_out = grad_gated * long_out
    back_init = (zero_spec, jnp.zeros((blocks, spec_len, features_count), jnp.float32))
    own_grad_spec = transform(tail_pair, grad_long)
    state = back_init
    portions = (
        lax.all_gather(signal, "seq", axis=1, tiled=True),
        lax.all_gather(grad_long, "seq", axis=1, tiled=True),
    )
    offset = jnp.int32(0)
    for member in range(portions[0].shape[1] // block_len):
        lower = member * block_len
        signal_block = portions[0][:, lower : lower + block_len]
        grad_block = portions[1][:, lower : lower + block_len]
        source = offset // block_len + member
        grad_sig, grad_filter = state
        lag_filter = position - source
        index_filter = jnp.clip(lag_filter, 0, blocks - 1)
        term = jnp.sum(spec_conj_mul(transform(head_pair, signal_block), own_grad_spec), axis=0)
        current = lax.dynamic_index_in_dim(grad_filter, index_filter, 0, keepdims=False)
        grad_filter = lax.dynamic_update_index_in_dim(
            grad_filter, current + jnp.where(lag_filter >= 0, term, 0.0), index_filter, 0
        )
        lag_signal = source - position
        grad_sig = grad_sig + jnp.where(
            lag_signal >= 0,
            spec_conj_mul(filter_at(lag_signal)[None], transform(tail_pair, grad_block)),
            0.0,
        )
        state = (grad_sig, grad_filter)
    grad_sig_spec, grad_filter_spec = state
    grad_conv = jnp.einsum(
        "nf,sfd->snd",
        inverse_table[:block_len],
        grad_sig_spec,
        precision=highest,
        preferred_element_type=jnp.float32,
    )
    grad_signal = grad_conv + conv_bias * grad_long_wide
    grad_bias = jnp.sum(grad_long_wide * signal_wide, axis=(0, 1))
    grad_segments = jnp.einsum(
        "nf,kfd->knd",
        inverse_table,
        grad_filter_spec,
        precision=highest,
        preferred_element_type=jnp.float32,
    )
    grad_taps = grad_segments[:, block_len:] + jnp.concatenate(
        [grad_segments[1:, :block_len], zero_block], axis=0
    )
    grad_first, grad_second, grad_third = filter_back(grad_taps.reshape(seq_len, features_count))
    grad_mixed = jnp.concatenate(
        [grad_gate_out, grad_signal * values, grad_signal * gate_in], axis=-1
    )
    later = from_behind(grad_mixed[:, :2], "seq", -1)
    grad_ext = jnp.concatenate([grad_mixed, later], axis=1)
    grad_proj = (
        kernel[0] * grad_ext[:, :block_len]
        + kernel[1] * grad_ext[:, 1 : block_len + 1]
        + kernel[2] * grad_ext[:, 2:]
    ).astype(jnp.bfloat16)
    grad_kernel = jnp.stack(
        [
            jnp.sum(grad_mixed * extended[:, 2:], axis=(0, 1)),
            jnp.sum(grad_mixed * extended[:, 1 : block_len + 1], axis=(0, 1)),
            jnp.sum(grad_mixed * extended[:, :block_len], axis=(0, 1)),
        ]
    )
    grad_in_w = jnp.einsum("std,ste->de", normed1, grad_proj, preferred_element_type=jnp.float32)
    grad_norm1 = jnp.einsum("ste,de->std", grad_proj, w_in, preferred_element_type=jnp.float32)
    grad_inputs, grad_gain1 = norm1_back(grad_norm1)
    tokens_grad = grad_res + grad_inputs
    filter_sums = lax.psum((grad_first, grad_second), ("batch", "seq"))
    summed_all = (
        lax.psum_scatter(grad_gain1, ("batch", "seq"), scatter_dimension=0, tiled=True),
        lax.psum_scatter(grad_in_w, ("batch", "seq"), scatter_dimension=0, tiled=True),
        lax.psum_scatter(grad_kernel, ("batch", "seq"), scatter_dimension=1, tiled=True),
        lax.psum_scatter(grad_third, ("batch", "seq"), scatter_dimension=1, tiled=True),
        lax.psum_scatter(grad_bias, ("batch", "seq"), scatter_dimension=0, tiled=True),
        lax.psum_scatter(grad_out_w, ("batch", "seq"), scatter_dimension=0, tiled=True),
        lax.psum_scatter(grad_gain2, ("batch", "seq"), scatter_dimension=0, tiled=True),
        lax.psum_scatter(grad_up, ("batch", "seq"), scatter_dimension=0, tiled=True),
        lax.psum_scatter(grad_down, ("batch", "seq"), scatter_dimension=0, tiled=True),
    )
    (
        summed_gain1,
        summed_in,
        summed_kernel,
        summed_third,
        summed_bias,
        summed_out,
        summed_gain2,
        summed_up,
        summed_down,
    ) = summed_all
    return (
        layer_out,
        tokens_grad,
        summed_gain1,
        summed_in,
        summed_kernel,
        filter_sums[0],
        filter_sums[1],
        summed_third,
        summed_bias,
        summed_out,
        summed_gain2,
        summed_up,
        summed_down,
    )


def solution(mesh):
    return jax.shard_map(
        on_device,
        mesh=mesh,
        in_specs=(
            P("batch", "seq", None),
            P(),
            P(),
            P(),
            P(),
            P(),
            P(),
            P(),
            P(),
            P(),
            P(),
            P(),
            P(),
            P("batch", "seq", None),
        ),
        out_specs=(
            P("batch", "seq", None),
            P("batch", "seq", None),
            P(("batch", "seq")),
            P(("batch", "seq"), None),
            P(None, ("batch", "seq")),
            P(),
            P(),
            P(None, ("batch", "seq")),
            P(("batch", "seq")),
            P(("batch", "seq"), None),
            P(("batch", "seq")),
            P(("batch", "seq"), None),
            P(("batch", "seq"), None),
        ),
        check_vma=False,
    )
```

profile of v0, /device:TPU:1, one launch (start us, length us, event | category | flops | bytes accessed | tf_op | source)
XLA Modules:
  0.0 1563.1 jit_solution(7769443400943547877)
XLA Ops:
  10.5 4.9 fusion.42
  15.5 4.2 collective-permute-start
  19.7 4.1 sine_negate_fusion
  24.3 1.9 fusion.159
  26.2 1.9 fusion.160
  28.8 4.5 multiply_convert_fusion.1
  33.6 8.2 fusion.57
  41.8 1.9 maximum_convert_fusion
  45.4 1.7 copy-done.16
  48.1 3.7 subtract_convert_fusion.1
  51.7 3.2 maximum_multiply_fusion
  54.9 12.7 convolution_add_fusion
  67.7 29.0 %dynamic-slice_bitcast_fusion = (f32[1,1024,1024]{2,1,0:T(8,128)}, f32[1,1024,1024]{2,1,0:T(8,128)}, f32[1,1024,1024]{2,1,0:T(8,128)}, f32[1,1024,1024]{2,1,0:T(...) fusion(f32[4,1024,1024]{1,2,0:T(8,128)} %convolution_add_fusion, ...), kind=kLoop, calls=%fused_computation.60 | loop fusion | bytes 67108896 | tf_op jit(solution)/shard_map/jit(dynamic_index_in_dim)/dynamic_slice | solution.py:157
  96.7 1.9 fusion.118
  99.4 2.7 copy-done.25
  102.1 1.4 subtract_bitcast_fusion.7
  105.0 2.7 copy-done.24
  107.8 1.4 subtract_bitcast_fusion.6
  110.7 2.7 copy-done.23
  113.4 2.5 subtract_bitcast_fusion.5
  117.3 2.7 copy-done.22
  120.1 3.0 subtract_bitcast_fusion.4
  123.1 7.6 fusion.72
  132.1 5.9 fusion.153
  138.0 9.4 fusion.7
  147.5 7.3 fusion.98
  155.5 2.6 fusion.86
  158.7 1.8 fusion.108
  160.6 2.9 add_bitcast_fusion
  163.8 1.8 copy-done.11
  165.7 6.9 multiply_add_fusion.2
  172.5 8.0 broadcast_in_dim.38
  180.6 2.6 fusion.35
  185.6 7.3 multiply_add_fusion.1
  192.8 7.1 fusion.37
  199.9 5.6 fusion.39
  205.5 5.8 fusion.41
  211.3 32.0 %convolution_bitcast_fusion = f32[4,512,1024]{2,1,0:T(8,128)S(1)} fusion(f32[4,1024,1024]{2,1,0:T(8,128)} %fusion.41, f32[512,512]{1,0:T(8,128)S(1)} %copy-done.30, f32[512,512]{1,0:T(8,128)S(1)} %copy-done.33), kind=kOutput, calls=%fused_computation.81 | convolution fusion | flops 25770852352 | bytes 27262976 | tf_op jit(solution)/shard_map/nf,kfd->knd/dot_general | solution.py:243
  243.6 2.9 slice_add_fusion
  246.5 1.9 fusion.122
  253.1 1.4 copy-done.20
  262.3 2.3 add_bitcast_fusion.9
  264.5 7.3 slice_multiply_fusion.3
  272.2 1.6 collective-permute-start.1
  274.0 2.6 bitcast_multiply_fusion
  278.5 3.0 multiply_reduce_fusion.2
  281.6 1.7 copy.33
  283.3 9.7 fusion.163
  293.2 2.7 fusion.164
  297.3 6.5 fusion.147
  305.1 10.0 fusion.151
  316.1 10.8 fusion.111
  327.9 6.9 convolution_multiply_fusion.1
  334.9 1.9 convolution_multiply_fusion
  337.6 7.2 fusion.79
  344.8 2.2 fusion.88
  348.6 41.9 %all-reduce.5 = (f32[1024]{0:T(1024)S(1)}, f32[33,64]{1,0:T(8,128)}, f32[64,64]{1,0:T(8,128)}, f32[1024]{0:T(1024)S(1)}, f32[1024]{0:T(1024)S(1)}) all-reduce(f32[1024]{0:T(1024)S(1)} %get-tuple-element.18, f32[33,64]{1,0:T(8,128)S(1)} %fusion.126, ...), channel_id=2, replica_groups=mesh['batch'=8,'seq'=4] {'batch','seq'}, use_global_device_ids=true, to_apply=%region_9.10.clone | all-reduce | flops 9280 | bytes 74240
  392.3 3.0 add_add_fusion.2
  395.3 1.4 copy.34
  396.7 116.6 %reduce-scatter.11.cloned.1.call-done = f32[64,32]{0,1:T(8,128)} async-done(((f32[64,1024]{0,1:T(8,128)}), f32[64,32]{0,1:T(8,128)}) %reduce-scatter.11.cloned.1.call-update) | async-done | bytes 8208 | tf_op jit(solution)/shard_map/reduce_scatter | solution.py:280
  513.3 146.6 %reduce-scatter.13.cloned.1.call-done = f32[32,1024]{1,0:T(8,128)} async-done(((f32[1024,1024]{1,0:T(8,128)}), f32[32,1024]{1,0:T(8,128)}) %reduce-scatter.13.cloned.1.call-update) | async-done | bytes 131088 | tf_op jit(solution)/shard_map/reduce_scatter | solution.py:282
  659.9 164.6 %reduce-scatter.9.cloned.1.call-done = f32[32,3072]{1,0:T(8,128)} async-done(((f32[1024,3072]{1,0:T(8,128)}), f32[32,3072]{1,0:T(8,128)}) %reduce-scatter.9.cloned.1.call-update) | async-done | bytes 393232 | tf_op jit(solution)/shard_map/reduce_scatter | solution.py:278
  824.6 366.4 %reduce-scatter.15.cloned.1.call-done = f32[32,4096]{1,0:T(8,128)} async-done(((f32[1024,4096]{1,0:T(8,128)}), f32[32,4096]{1,0:T(8,128)}) %reduce-scatter.15.cloned.1.call-update) | async-done | bytes 524304 | tf_op jit(solution)/shard_map/reduce_scatter | solution.py:284
  1191.0 365.1 %reduce-scatter.17.cloned.1.call-done = f32[128,1024]{1,0:T(8,128)} async-done(((f32[4096,1024]{1,0:T(8,128)}), f32[128,1024]{1,0:T(8,128)}) %reduce-scatter.17.cloned.1.call-update) | async-done | bytes 524304 | tf_op jit(solution)/shard_map/reduce_scatter | solution.py:285
  (283 shorter events, 41.5 us)
Async XLA Ops:
  7.2 123.7 %copy-start = (bf16[1024,1024]{1,0:T(8,128)(2,1)S(1)}, bf16[1024,1024]{1,0:T(8,128)(2,1)}, u32[]{:S(2)}) copy-start(bf16[1024,1024]{1,0:T(8,128)(2,1)} %param.23) | copy-start | bytes 6291460
  7.2 89.5 %all-gather.3.cloned.1.call-start = ((), (), s32[]{:S(2)}) async-start(), calls=%async_computation.6 | async-start | bytes 2621440 | tf_op jit(solution)/shard_map/all_gather | solution.py:163
  8.6 6.9 copy-start.90
  10.5 4.9 copy-start.86
  10.5 13.4 copy-start.103
  10.5 13.7 copy-start.92
  10.5 15.7 %copy-start.78 = (f32[64,64]{1,0:T(8,128)S(1)}, f32[64,64]{1,0:T(8,128)}, u32[]{:S(2)}) copy-start(f32[64,64]{1,0:T(8,128)} %param.19) | copy-start | bytes 49156
  15.5 17.9 %copy-start.65 = (bf16[1,256,3072]{2,1,0:T(8,128)(2,1)}, bf16[1,256,3072]{2,1,0:T(8,128)(2,1)S(1)}, u32[]{:S(2)}) copy-start(bf16[1,256,3072]{2,1,0:T(8,128)(2,1)S(1)} %fusion.42) | copy-start | bytes 4718596
  15.5 13.4 copy-start.74
  15.5 26.3 %collective-permute-start = (bf16[1,2,3072]{2,1,0:T(2,128)(2,1)S(1)}, bf16[1,2,3072]{2,1,0:T(2,128)(2,1)S(1)}, u32[]{:S(2)}, u32[]{:S(2)}) collective-permute-start(bf16[1,2,3072]{2,1,0:T(2,128)(2,1)S(1)} %slice.130), channel_id=1, source_target_pairs={{0,1},{1,2},{2,3},{4,5},{5,6},{6,7},{8,9},{9,10},{10,11},{12,13},{... | collective-permute-start | bytes 36872 | tf_op jit(solution)/shard_map/ppermute | solution.py:13
  19.7 8.4 copy-start.88
  19.7 13.6 copy-start.93
  23.9 9.7 copy-start.28
  23.9 9.7 copy-start.31
  23.9 9.6 copy-start.95
  28.8 4.7 copy-start.85
  33.4 8.4 copy-start.47
  33.5 8.3 copy-start.49
  33.6 10.1 copy-start.79
  33.6 10.1 copy-start.81
  33.6 10.1 copy-start.83
  48.0 198.5 %all-gather.5.cloned.1.call-start = ((), (), s32[]{:S(2)}) async-start(), calls=%async_computation.7 | async-start | bytes 2621440 | tf_op jit(solution)/shard_map/all_gather | solution.py:210
  48.0 6.9 copy-start.29
  48.1 6.9 copy-start.32
  48.1 6.9 copy-start.48
  110.7 5.2 copy-start.10
  117.3 5.8 copy-start.8
  123.1 7.6 copy-start.17
  123.1 7.8 copy-start.12
  130.9 7.1 copy-start.45
  131.8 23.1 %copy-start.14 = (f32[1,256,1024]{2,1,0:T(8,128)}, f32[1,256,1024]{2,1,0:T(8,128)S(1)}, u32[]{:S(2)}) copy-start(f32[1,256,1024]{2,1,0:T(8,128)S(1)} %get-tuple-element.85) | copy-start | bytes 3145732
  132.1 6.0 copy-start.55
  138.0 9.5 copy-start.52
  147.5 7.4 copy-start.62
  158.2 237.1 %reduce-scatter.19.cloned.1.call-start = ((), (), s32[]{:S(2)}) async-start(), calls=%async_computation.13 | async-start | bytes 1622016
  160.6 5.1 copy-start.11
  172.5 8.0 copy-start.41
  172.5 8.0 copy-start.42
  180.5 5.0 copy-start.9
  192.8 7.1 copy-start.38
  199.9 5.6 copy-start.39
  199.9 5.6 copy-start.40
  205.5 5.8 copy-start.30
  205.5 5.8 copy-start.33
  264.5 7.3 copy-start.26
  272.2 4.8 collective-permute-start.1
  283.2 9.9 copy-start.46
  283.3 9.9 copy-start.58
  283.3 230.0 %reduce-scatter.11.cloned.1.call-start = ((), (), s32[]{:S(2)}) async-start(), calls=%async_computation.9 | async-start | bytes 540672 | tf_op jit(solution)/shard_map/reduce_scatter | solution.py:280
  293.1 366.8 %reduce-scatter.13.cloned.1.call-start = ((), (), s32[]{:S(2)}) async-start(), calls=%async_computation.10 | async-start | bytes 4325376 | tf_op jit(solution)/shard_map/reduce_scatter | solution.py:282
  295.9 528.6 %reduce-scatter.9.cloned.1.call-start = ((), (), s32[]{:S(2)}) async-start(), calls=%async_computation.8 | async-start | bytes 12976128 | tf_op jit(solution)/shard_map/reduce_scatter | solution.py:278
  303.9 887.1 %reduce-scatter.15.cloned.1.call-start = ((), (), s32[]{:S(2)}) async-start(), calls=%async_computation.11 | async-start | bytes 17301504 | tf_op jit(solution)/shard_map/reduce_scatter | solution.py:284
  315.1 1241.0 %reduce-scatter.17.cloned.1.call-start = ((), (), s32[]{:S(2)}) async-start(), calls=%async_computation.12 | async-start | bytes 17301504 | tf_op jit(solution)/shard_map/reduce_scatter | solution.py:285
  326.9 8.0 copy-start.69
  326.9 9.8 copy-start.71
  327.0 9.8 copy-start.73
  327.0 9.8 copy-start.89
  327.0 10.2 copy-start.61
  327.9 9.6 copy-start.53
  327.9 16.8 %slice-start = ((s8[6291456]{0:T(1024)(128)(4,1)}), s8[4194304]{0:T(1024)(128)(4,1)S(1)}, s32[]{:S(2)}) async-start(s8[6291456]{0:T(1024)(128)(4,1)} %bitcast.276), calls=%async_computation.14 | async-start | bytes 8388608
  337.5 7.2 copy-start.51
  337.5 7.2 slice-start.1
  344.8 47.5 %copy-start.99 = (f32[256]{0:T(256)S(1)}, f32[256]{0:T(256)}, u32[]{:S(2)}) copy-start(f32[256]{0:T(256)} %copy-done.98) | copy-start | bytes 3076
  344.8 1211.3 %copy-start.1 = (bf16[1024,1024]{1,0:T(8,128)(2,1)S(1)}, bf16[1024,1024]{1,0:T(8,128)(2,1)}, u32[]{:S(2)}) copy-start(bf16[1024,1024]{1,0:T(8,128)(2,1)} %param.23) | copy-start | bytes 6291460
  (53 other events, 121.7 us)
Sparse Core Ops, SparseCore 0:
  48.1 46.4 all-gather.2
  158.3 45.6 all-gather.4
  283.4 96.9 reduce-scatter.18
  383.1 130.2 reduce-scatter.10
  516.1 143.7 reduce-scatter.12
  667.4 157.0 reduce-scatter.8
  827.4 363.5 reduce-scatter.14
  1193.8 362.1 reduce-scatter.16
where the time goes:
time: 1570 us; the launch traced here: 1560 us
  waiting for transfers between devices  1160 us (74%)
  matrix products  185 us (12%)
  other arithmetic  80.2 us (5%)
  local copies, waits for them, and re-layouts  74 us (5%)
  blocking collectives  41.9 us (3%)
  between operations  15.8 us (1%)
    reduce_scatter x1, waiting for transfers between devices, on_device(): lax.psum_scatter(grad_up, ('batch', 'seq'), scatter_dimension=0, tiled=True)  366 us
    reduce_scatter x1, waiting for transfers between devices, on_device(): lax.psum_scatter(grad_down, ('batch', 'seq'), scatter_dimension=0, tiled=...  365 us
    reduce_scatter x1, waiting for transfers between devices, on_device(): lax.psum_scatter(grad_in_w, ('batch', 'seq'), scatter_dimension=0, tiled=...  165 us
    reduce_scatter x1, waiting for transfers between devices, on_device(): lax.psum_scatter(grad_out_w, ('batch', 'seq'), scatter_dimension=0, tiled...  147 us
    reduce_scatter x1, waiting for transfers between devices, on_device(): lax.psum_scatter(grad_third, ('batch', 'seq'), scatter_dimension=1, tiled...  117 us
    unnamed x1, blocking collectives  41.9 us
    unnamed x219, local copies, waits for them, and re-layouts  36.6 us
    dot_general x1, matrix products, on_device(): jnp.einsum('nf,kfd->knd', inverse_table, grad_filter_spec, precision=high...  32 us
  transfers between devices with their start and end apart: 10, of which 6 were waited for; matrix products, arithmetic and copies ran while one was open for 14% of the time, Pallas kernels for 0%

commit v1 on v0

v1 whole, which is shorter than its diff:
```python
import math

import jax
import jax.numpy as jnp
import ml_dtypes
import numpy as np
from jax import lax
from jax.experimental import pallas as pl
from jax.experimental.pallas import tpu as pltpu
from jax.sharding import PartitionSpec as P

F32 = jnp.float32
BF16 = jnp.bfloat16
HIGHEST = lax.Precision.HIGHEST
GELU_SCALE = math.sqrt(2.0 / math.pi)
GELU_CUBIC = 0.044715


def dot(left, right, contract, out=F32, precision=None):
    return lax.dot_general(
        left, right, (contract, ((), ())), precision=precision, preferred_element_type=F32
    ).astype(out)


def mm(left, right, **kw):
    return dot(left, right, ((1,), (0,)), **kw)


def mm_nt(left, right, **kw):
    return dot(left, right, ((1,), (1,)), **kw)


def mm_tn(left, right, **kw):
    return dot(left, right, ((0,), (0,)), **kw)


def shifted(value, axis, steps):
    count = lax.axis_size(axis)
    first, last = (max(0, -steps), min(count, count - steps))
    return lax.ppermute(value, axis, [(source, source + steps) for source in range(first, last)])


def exchange(value, axis, bit):
    count = lax.axis_size(axis)
    return lax.ppermute(value, axis, [(at, at ^ (1 << bit)) for at in range(count)])


def bits_of(axis):
    return lax.axis_size(axis).bit_length() - 1


def stage_order(swap):
    batch_bits, seq_bits = bits_of("batch"), bits_of("seq")
    rest = list(range(1, batch_bits))
    half = len(rest) // 2
    if swap:
        rest = rest[half:] + rest[:half]
    return [("batch", bit) for bit in [0] + rest] + [("seq", bit) for bit in range(seq_bits)]


def scatter_sum(partial, swap=False, wire=BF16):
    batch_bits, seq_bits = bits_of("batch"), bits_of("seq")
    dims = [("batch", bit) for bit in reversed(range(batch_bits))]
    dims += [("seq", bit) for bit in reversed(range(seq_bits))]
    rows = partial.shape[0] >> len(dims)
    value = partial.reshape((2,) * len(dims) + (rows,) + partial.shape[1:]).astype(wire)
    for axis, bit in stage_order(swap):
        at = dims.index((axis, bit))
        mine = (lax.axis_index(axis) >> bit) & 1
        keep = lax.dynamic_index_in_dim(value, mine, at, keepdims=False)
        send = lax.dynamic_index_in_dim(value, 1 - mine, at, keepdims=False)
        got = exchange(send, axis, bit)
        value = keep.astype(F32) + got.astype(F32)
        dims.pop(at)
        if dims:
            value = value.astype(wire)
    return value


def gather_batch(value):
    return lax.all_gather(value, "batch", axis=0, tiled=True)


def columns_batch(value):
    return lax.all_to_all(value, "batch", 1, 0, tiled=True)


def rows_sum(left_own, right_all):
    blocks = lax.axis_size("seq")
    part = mm_tn(left_own, right_all, out=BF16)
    got = lax.all_to_all(part.reshape(blocks, -1, part.shape[1]), "seq", 0, 0, tiled=True)
    return jnp.sum(got.astype(F32), axis=0)


def columns_sum(left_all, right_own):
    blocks, groups = lax.axis_size("seq"), lax.axis_size("batch")
    part = mm_tn(left_all, right_own, out=BF16)
    part = part.reshape(groups * blocks, -1, part.shape[1])
    got = lax.all_to_all(part, ("batch", "seq"), 0, 0, tiled=True)
    got = jnp.sum(got.reshape(groups, blocks, -1, part.shape[2]).astype(F32), axis=1)
    return got.transpose(1, 0, 2).reshape(got.shape[1], -1)


def all_sum(value):
    for axis, bit in stage_order(False):
        value = value + exchange(value, axis, bit)
    return value


def norm_parts(values):
    centered = values - jnp.mean(values, axis=-1, keepdims=True)
    inverse = lax.rsqrt(jnp.mean(centered * centered, axis=-1, keepdims=True) + 1e-05)
    return centered * inverse, inverse


def norm_back(grad, gain, xhat, inverse):
    scaled = grad * gain
    return (
        scaled
        - jnp.mean(scaled, axis=-1, keepdims=True)
        - xhat * jnp.mean(scaled * xhat, axis=-1, keepdims=True)
    ) * inverse


def transform_table(length):
    count = np.arange(length, dtype=np.int64)
    turns = (2 * count[:, None] + 1) * count[None, :] % (4 * length)
    angles = turns.astype(np.float64) * (2.0 * np.pi / (4 * length))
    table = np.concatenate([np.cos(angles), -np.sin(angles)], axis=0)
    return table.astype(np.float32).astype(ml_dtypes.bfloat16)


def lag_features(emb, length):
    bands = (emb - 1) // 2
    lag = np.arange(length, dtype=np.float64)
    freq = 1e-4 + np.arange(bands, dtype=np.float64) * ((bands - 1 - 1e-4) / (bands - 1))
    phases = (lag * (2.0 * np.pi / length))[:, None] * freq[None, :]
    return np.concatenate(
        [(lag / (length - 1))[:, None], np.cos(phases), -np.sin(phases)], axis=1
    ).astype(np.float32)


def to_channels(value):
    return lax.all_to_all(value, "seq", 1, 0, tiled=True)


def to_tokens(value):
    return lax.all_to_all(value, "seq", 0, 1, tiled=True)


def plain_layer(
    tokens,
    norm_gain1,
    w_in,
    short_kernel,
    filt_w1,
    filt_w2,
    filt_w3,
    decay_rate,
    conv_bias,
    w_out,
    norm_gain2,
    w_up,
    w_down,
    cotangent,
):
    num_seqs, block_len, width = tokens.shape
    assert num_seqs == 1
    blocks = lax.axis_size("seq")
    position = lax.axis_index("seq")
    seq_len = block_len * blocks
    own = width // blocks
    table = jnp.asarray(transform_table(seq_len))
    features = jnp.asarray(lag_features(filt_w1.shape[0], seq_len))
    cot = cotangent[0]
    cot_all = gather_batch(cot)
    inputs = tokens[0].astype(F32)

    xhat1, inverse1 = norm_parts(inputs)
    normed1 = (xhat1 * norm_gain1).astype(BF16)
    normed1_all = gather_batch(normed1)
    projected = mm(normed1, w_in, out=BF16)
    earlier = shifted(projected[block_len - 2 :], "seq", 1)
    extended = jnp.concatenate([earlier, projected], axis=0).astype(F32)
    taps3 = short_kernel.astype(F32)
    lags = [extended[2 - lag : 2 - lag + block_len] for lag in range(3)]
    mixed = taps3[0] * lags[0] + taps3[1] * lags[1] + taps3[2] * lags[2]
    gate_out = mixed[:, :width]
    gate_in = mixed[:, width : 2 * width]
    values = mixed[:, 2 * width :]
    signal = (values * gate_in).astype(BF16)

    w3_own = lax.dynamic_slice_in_dim(filt_w3, position * own, own, 1)
    decay_own = lax.dynamic_slice_in_dim(decay_rate, position * own, own, 0)
    angle1 = mm(features, filt_w1, precision=HIGHEST)
    hidden1, slope1 = jnp.sin(angle1), jnp.cos(angle1)
    angle2 = mm(hidden1, filt_w2, precision=HIGHEST)
    hidden2, slope2 = jnp.sin(angle2), jnp.cos(angle2)
    lag_index = jnp.arange(seq_len).astype(F32)
    fading = jnp.exp(-decay_own[None, :] * lag_index[:, None])
    taps = (mm(hidden2, w3_own, precision=HIGHEST) * fading).astype(BF16)
    taps_spec = mm(table, taps)
    taps_re, taps_im = taps_spec[:seq_len], taps_spec[seq_len:]

    signal_spec = mm(table, to_channels(signal))
    signal_re, signal_im = signal_spec[:seq_len], signal_spec[seq_len:]
    scale = 1.0 / seq_len

    def inverse_of(real, imag):
        both = (jnp.concatenate([real, imag], axis=0) * scale).astype(BF16)
        return mm_tn(table, both)

    conv = inverse_of(
        taps_re * signal_re - taps_im * signal_im, taps_re * signal_im + taps_im * signal_re
    )
    long_out = to_tokens(conv.astype(BF16)).astype(F32) + conv_bias * signal.astype(F32)
    gated = (long_out * gate_out).astype(BF16)
    gated_all = gather_batch(gated)
    residual1 = inputs + mm(gated, w_out)
    xhat2, inverse2 = norm_parts(residual1)
    normed2 = (xhat2 * norm_gain2).astype(BF16)
    normed2_all = gather_batch(normed2)
    pre = mm(normed2, w_up)
    bent = jnp.tanh(GELU_SCALE * (pre + GELU_CUBIC * pre * pre * pre))
    hidden = (0.5 * pre * (1.0 + bent)).astype(BF16)
    layer_out = (residual1 + mm(hidden, w_down)).astype(BF16)

    slope = 0.5 * (1.0 + bent) + 0.5 * pre * (1.0 - bent * bent) * GELU_SCALE * (
        1.0 + 3.0 * GELU_CUBIC * pre * pre
    )
    grad_pre = (mm_nt(cot, w_down) * slope).astype(BF16)
    grad_w_down = rows_sum(columns_batch(hidden), cot_all)
    grad_w_up = columns_sum(normed2_all, columns_batch(grad_pre))
    grad_norm2 = mm_nt(grad_pre, w_up)
    grad_gain2 = jnp.sum(grad_norm2 * xhat2, axis=0)
    grad_res = cot.astype(F32) + norm_back(grad_norm2, norm_gain2, xhat2, inverse2)
    grad_branch = grad_res.astype(BF16)
    grad_w_out = columns_sum(gated_all, columns_batch(grad_branch))
    grad_gated = mm_nt(grad_branch, w_out)
    grad_long = (grad_gated * gate_out).astype(BF16)
    grad_gate_out = grad_gated * long_out
    grad_bias = jnp.sum(grad_long.astype(F32) * signal.astype(F32), axis=0)

    grad_spec = mm(table, to_channels(grad_long))
    grad_re, grad_im = grad_spec[:seq_len], grad_spec[seq_len:]
    grad_conv = inverse_of(
        taps_re * grad_re + taps_im * grad_im, taps_re * grad_im - taps_im * grad_re
    )
    grad_signal = to_tokens(grad_conv.astype(BF16)).astype(F32) + conv_bias * grad_long.astype(F32)
    grad_taps = inverse_of(
        signal_re * grad_re + signal_im * grad_im, signal_re * grad_im - signal_im * grad_re
    )
    grad_filt = grad_taps * fading
    grad_w3_own = mm_tn(hidden2, grad_filt)
    grad_angle2 = mm_nt(grad_filt, w3_own) * slope2
    grad_w2 = mm_tn(hidden1, grad_angle2)
    grad_angle1 = mm_nt(grad_angle2, filt_w2) * slope1
    grad_w1 = mm_tn(features, grad_angle1)

    grad_mixed = jnp.concatenate(
        [grad_gate_out, grad_signal * values, grad_signal * gate_in], axis=1
    )
    later = shifted(grad_mixed[:2], "seq", -1)
    grad_ext = jnp.concatenate([grad_mixed, later], axis=0)
    grad_proj = (
        taps3[0] * grad_ext[:block_len]
        + taps3[1] * grad_ext[1 : block_len + 1]
        + taps3[2] * grad_ext[2:]
    ).astype(BF16)
    grad_short = jnp.stack([jnp.sum(grad_mixed * lag, axis=0) for lag in lags])
    grad_w_in = columns_sum(normed1_all, columns_batch(grad_proj))
    grad_norm1 = mm_nt(grad_proj, w_in)
    grad_gain1 = jnp.sum(grad_norm1 * xhat1, axis=0)
    tokens_grad = grad_res + norm_back(grad_norm1, norm_gain1, xhat1, inverse1)

    return layer_out[None], tokens_grad[None], small_sums(
        grad_gain1, grad_bias, grad_gain2, grad_short, grad_w1, grad_w2, grad_w3_own
    ), (grad_w_in, grad_w_out, grad_w_up, grad_w_down)


MESH = pl.DeviceIdType.MESH
KERNEL_VMEM = 63 * 1024 * 1024


def symmetric_tables(length):
    odd = 2 * np.arange(length, dtype=np.int64) + 1
    angles = (odd[:, None] * odd[None, :] % (8 * length)).astype(np.float64) * (
        np.pi / (4 * length)
    )
    phase = odd.astype(np.float64) * (np.pi / (4 * length))
    tables = [np.cos(angles), np.sin(angles)]
    tables = [t.astype(np.float32).astype(ml_dtypes.bfloat16) for t in tables]
    return tables, np.stack([np.cos(phase), np.sin(phase)], axis=1).astype(np.float32)


def sin_cos(x):
    turns = jnp.floor(x * (2.0 / np.pi) + 0.5)
    rest = ((x - turns * 1.5703125) - turns * 4.837512969970703e-4) - turns * 7.54978995489188e-8
    square = rest * rest
    sine = rest + rest * square * (
        -1.6666654611e-1 + square * (8.3321608736e-3 - square * 1.9515295891e-4)
    )
    cosine = (1.0 - 0.5 * square) + square * square * (
        4.166664568298827e-2 + square * (-1.388731625493765e-3 + square * 2.443315711809948e-5)
    )
    quarter = turns - 4.0 * jnp.floor(turns * 0.25)
    odd = (quarter == 1.0) | (quarter == 3.0)
    sin_sign = jnp.where(quarter >= 2.0, -1.0, 1.0)
    cos_sign = jnp.where((quarter == 1.0) | (quarter == 2.0), -1.0, 1.0)
    return sin_sign * jnp.where(odd, cosine, sine), cos_sign * jnp.where(odd, sine, cosine)


class Named:
    def __init__(self, names, refs):
        assert len(names) == len(refs)
        for name, ref in zip(names, refs):
            setattr(self, name, ref)


def kernel_plan(groups, blocks, tokens, width, hidden, filt, emb):
    length = tokens * blocks
    own = width // blocks
    ffc = hidden // groups
    share = width // groups
    rows_out = share // blocks
    inc = 3 * share
    chips = groups // 2
    down_rows = ffc // blocks
    net_at = -(-emb // 8) * 8
    net_rows = net_at + filt
    peers, zpeers = groups - 1, blocks - 1
    vm, hbm = pltpu.VMEM, pl.ANY
    inputs = dict(
        tokens=hbm, cot=hbm, w_in=hbm, w_out=hbm, w_up=hbm, w_down=hbm,
        cosine=hbm, sine=hbm, filt_w3=hbm, decay=hbm,
        gain1=vm, gain2=vm, bias=vm, short=vm, filt_w1=vm, filt_w2=vm,
        features_t=vm, phase=vm,
    )
    outputs = dict(
        layer_out=((tokens, width), BF16, hbm),
        tokens_grad=((tokens, width), F32, hbm),
        grad_w_in=((rows_out, 3 * width), F32, hbm),
        grad_w_out=((rows_out, width), F32, hbm),
        grad_w_up=((rows_out, hidden), F32, hbm),
        grad_w_down=((ffc // blocks, width), F32, hbm),
        grad_gain1=((1, rows_out), F32, vm),
        grad_gain2=((1, rows_out), F32, vm),
        grad_bias=((1, rows_out), F32, vm),
        grad_short=((3, 3 * rows_out), F32, vm),
        grad_w1=((emb, filt), F32, vm),
        grad_w2=((filt, filt), F32, vm),
        grad_w3=((filt, rows_out), F32, vm),
        cot_land=((2, groups // 2 * tokens, width), BF16, hbm),
        n1_land=((groups, width, tokens), BF16, hbm),
        n2_land=((groups, width, tokens), BF16, hbm),
    )
    dma = pltpu.SemaphoreType.DMA
    scratch = dict(
        tok=vm((tokens, width), BF16), cotv=vm((tokens, width), BF16),
        mean1=vm((tokens, 128), F32), inv1=vm((tokens, 128), F32),
        n1=vm((tokens, width), BF16), turn=vm((width, tokens), BF16),
        gated_turn=vm((width, tokens), BF16), gated_pair=vm((width // 2, 2 * tokens), BF16),
        hid_buf=vm((tokens, ffc), BF16), gmix=vm((tokens + 8, 3 * width), F32),
        win=vm((3, width, width), BF16), wout=vm((width, width), BF16),
        cs=vm((length, length), BF16), sn=vm((length, length), BF16),
        ext=vm((tokens + 16, 3 * width), BF16),
        halo_out=vm((16, 3 * width), BF16), halo_in=vm((16, 3 * width), BF16),
        gate_out=vm((tokens, width), F32),
        sig=vm((tokens, width), BF16), chan=vm((length, own), BF16),
        w3=vm((filt, own), F32), fade=vm((1, own), F32),
        h1=vm((filt, length), F32), s1=vm((filt, length), F32),
        h2=vm((filt, length), F32), s2=vm((filt, length), F32),
        sum_gain1=vm((1, width), F32), sum_gain2=vm((1, width), F32),
        sum_bias=vm((1, width), F32), sum_short=vm((3, 3 * width), F32),
        small_send=vm((groups, 16, share), F32), small_land=vm((groups, 16, share), F32),
        small_sum=vm((16, share), F32), small_z=vm((zpeers, 16, share), F32),
        short_all=vm((8, inc), F32),
        w12=vm((net_rows, 128), F32), w12_z=vm((zpeers, net_rows, 128), F32),
        w12_sum=vm((net_rows, 128), F32), w12_plane=vm((peers, net_rows, 128), F32),
        sum_w3=vm((filt, own), F32), w3_land=vm((peers, filt // groups, own), F32),
        w3_part=vm((filt // groups, own), F32), w3_all=vm((blocks, filt, own), F32),
        hre=vm((length, own), F32), him=vm((length, own), F32),
        xre=vm((length, own), F32), xim=vm((length, own), F32),
        yre=vm((length, own), BF16), yim=vm((length, own), BF16),
        qre=vm((length, own), BF16), qim=vm((length, own), BF16),
        conv_out=vm((length, own), BF16), conv_in=vm((blocks, tokens, own), BF16),
        long=vm((tokens, width), F32), half=vm((tokens, width), BF16),
        res=vm((tokens, width), F32), xhat2=vm((tokens, width), F32),
        inv2=vm((tokens, 128), F32), gn2=vm((tokens, width), F32),
        gres=vm((tokens, width), F32),
        hid_send=vm((groups, ffc, tokens), BF16), hid_own=vm((ffc, groups * tokens), BF16),
        pre_send=vm((groups, tokens, ffc), BF16), pre_own=vm((groups * tokens, ffc), BF16),
        gbr_pair=vm((2 * tokens, width), BF16),
        glong=vm((tokens, width), BF16),
        gproj=vm((tokens, 3 * width), BF16), gproj_own=vm((groups * tokens, inc), BF16),
        down_send=vm((2, down_rows, width), BF16), down_land=vm((2, down_rows, width), BF16),
        down_next=vm((down_rows, width), BF16), down_last=vm((down_rows, width), BF16),
        down_own=vm((down_rows, width), F32),
        up_send=vm((2, own, ffc), BF16), up_land=vm((2, own, ffc), BF16),
        up_next=vm((own, ffc), BF16), up_last=vm((own, ffc), BF16), up_own=vm((own, ffc), F32),
        in_send=vm((2, own, inc), BF16), in_land=vm((2, own, inc), BF16),
        in_next=vm((own, inc), BF16), in_last=vm((own, inc), BF16), in_own=vm((own, inc), F32),
        out_send=vm((chips - 1, share, width), BF16), out_land=vm((chips - 1, share, width), BF16),
        out_own=vm((share, width), F32),
        outz_send=vm((share, width), BF16), outz_land=vm((zpeers, rows_out, width), BF16),
        outz_own=vm((rows_out, width), F32),
        load_sem=dma((16,)),
        pool_sem=dma((groups,)),
        win_sem=dma((3,)),
        ffn_sem=dma((2, 2)),
        local_sem=dma((16,)),
        stage=vm((chips - 1, width, tokens), BF16), stage_sem=dma((chips - 1,)),
        ag_s=dma((3, groups - 1)), ag_r=dma((3, groups - 1)),
        halo_s=dma((2,)), halo_r=dma((2,)),
        za_s=dma((4, zpeers)), za_r=dma((4, zpeers)),
        pa_s=dma((3, peers)), pa_r=dma((3, peers)),
        cx_s=dma((2,)), cx_r=dma((2,)), wo_s=dma((2, chips - 1)), wo_r=dma((2, chips - 1)),
        rs_s=dma((3, 2)), rs_r=dma((3, 2)),
        sm_s=dma((4, peers)), sm_r=dma((4, peers)),
        sz_s=dma((3, zpeers)), sz_r=dma((3, zpeers)),
        tr_s=dma((2, peers)), tr_r=dma((2, peers)),
    )
    names = [*inputs, *outputs, *scratch]

    def kernel(*refs):
        r = Named(names, refs)
        b, z = lax.axis_index("batch"), lax.axis_index("seq")
        chip, core = lax.div(b, 2), lax.rem(b, 2)
        sibling = chip * 2 + (1 - core)
        sent = {}

        def group_at(step):
            return lax.rem(b + step, groups)

        def block_at(step):
            return lax.rem(z + step, blocks)

        def span(at, size):
            return pl.ds(pl.multiple_of(at * size, size), size)

        def remote(src, dst, send_sem, recv_sem, **where):
            return pltpu.make_async_remote_copy(
                src_ref=src, dst_ref=dst, send_sem=send_sem, recv_sem=recv_sem,
                device_id=where, device_id_type=MESH,
            )

        def send(key, copy):
            copy.start()
            sent.setdefault(key, []).append(copy)

        def drain(key):
            for copy in sent.pop(key):
                copy.wait_send()

        def tiles(size, total, body):
            def step(i, carry):
                body(pl.multiple_of(i * size, size))
                return carry

            lax.fori_loop(0, total // size, step, 0)

        def load(sem, src, dst):
            copy = pltpu.make_async_copy(src, dst, sem)
            copy.start()
            return copy

        def load_win(block):
            return load(r.win_sem.at[block], r.w_in.at[:, pl.ds(block * width, width)], r.win.at[block])

        load_tok = load(r.load_sem.at[0], r.tokens, r.tok)
        win_loads = [(block, load_win(block)) for block in (1, 2, 0)]
        load_cot = load(r.load_sem.at[5], r.cot, r.cotv)
        load_w3 = load(r.load_sem.at[1], r.filt_w3.at[:, span(z, own)], r.w3)
        load_fade = load(r.load_sem.at[2], r.decay.at[:, span(z, own)], r.fade)
        load_cs = load(r.load_sem.at[3], r.cosine, r.cs)
        load_sn = load(r.load_sem.at[4], r.sine, r.sn)
        load_wout = load(r.load_sem.at[6], r.w_out, r.wout)

        barrier = pltpu.get_barrier_semaphore()
        for step in range(1, groups):
            pl.semaphore_signal(barrier, inc=1, device_id={"batch": group_at(step)}, device_id_type=MESH)
        for step in range(1, blocks):
            pl.semaphore_signal(barrier, inc=1, device_id={"seq": block_at(step)}, device_id_type=MESH)
        pl.semaphore_wait(barrier, peers + zpeers)

        slots = [
            lambda at: r.cot_land.at[lax.div(at, chips), span(lax.rem(at, chips), tokens)],
            lambda at: r.n1_land.at[at],
            lambda at: r.n2_land.at[at],
        ]

        def gather_copy(k, at, src, slot, to):
            return remote(src, slot, r.ag_s.at[k, at], r.ag_r.at[k, at], batch=to)

        def gather_local(k, src):
            return pltpu.make_async_copy(src, slots[k](b), r.local_sem.at[k])

        def gather_start(k, src):
            for step in range(1, chips):
                to = lax.rem(chip + step, chips) * 2 + core
                send(("ag", k), gather_copy(k, step - 1, src, slots[k](b), to))
            send(("ag", k), gather_copy(k, chips - 1, src, slots[k](b), sibling))
            gather_local(k, src).start()

        def stage(k, step):
            if k == 0:
                return r.gproj.at[:, (step - 1) * width : step * width]
            return r.stage.at[step - 1]

        def gather_forward(k):
            if k >= 2:
                drain(("forward", k - 1))
            staged = []
            for step in range(1, chips):
                slot = slots[k](lax.rem(chip + chips - step, chips) * 2 + core)
                gather_copy(k, step - 1, slot, slot, sibling).wait_recv()
                staged.append((slot, load(r.stage_sem.at[step - 1], slot, stage(k, step))))
            for step, (slot, copy) in enumerate(staged, 1):
                copy.wait()
                source = stage(k, step)
                send(("forward", k), gather_copy(k, chips - 1 + step, source, slot, sibling))

        def gather_finish(k):
            for step in range(chips):
                slot = slots[k](lax.rem(chip + chips - step, chips) * 2 + 1 - core)
                gather_copy(k, chips - 1 + step, slot, slot, sibling).wait_recv()

        def turned(value_ref, out_ref):
            def body(at):
                tile = value_ref[:, pl.ds(at, share)].T
                group = lax.div(at, share)
                for block in range(blocks):
                    first = pl.multiple_of(block * own + group * rows_out, rows_out)
                    out_ref[pl.ds(first, rows_out), :] = tile[block * rows_out : (block + 1) * rows_out]

            tiles(share, width, body)

        def turned_by_core(value_ref, out_ref):
            def body(at):
                group = lax.div(at, share)
                out_ref[span(lax.rem(group, 2) * chips + lax.div(group, 2), share), :] = value_ref[
                    :, pl.ds(at, share)
                ].T

            tiles(share, width, body)

        load_cot.wait()
        gather_start(0, r.cotv)

        load_tok.wait()

        def norm1(at):
            rows = pl.ds(at, 32)
            x = r.tok[rows, :].astype(F32)
            xhat, inverse = norm_parts(x)
            r.mean1[rows, :] = jnp.broadcast_to(jnp.mean(x, axis=-1, keepdims=True), (32, 128))
            r.inv1[rows, :] = jnp.broadcast_to(inverse, (32, 128))
            r.n1[rows, :] = (xhat * r.gain1[...]).astype(BF16)

        tiles(32, tokens, norm1)
        for block, copy in win_loads:
            copy.wait()
            cols = slice(block * width, (block + 1) * width)
            proj = mm(r.n1[...], r.win[block], out=BF16)
            r.ext[16:, cols] = proj
            r.halo_out[:, cols] = proj[tokens - 16 :]
        halo = remote(r.halo_out, r.halo_in, r.halo_s.at[0], r.halo_r.at[0], seq=block_at(1))
        send("halo", halo)
        turned(r.n1, r.turn)
        gather_start(1, r.turn)

        def ffn_weights(at, slot):
            group = lax.rem(b + 1 + at, groups)
            where = span(slot, ffc)
            return (
                pltpu.make_async_copy(
                    r.w_up.at[:, span(group, ffc)], r.win.at[0, :, where], r.ffn_sem.at[slot, 0]
                ),
                pltpu.make_async_copy(
                    r.w_down.at[span(group, ffc)], r.win.at[1, where], r.ffn_sem.at[slot, 1]
                ),
            )

        for at in range(2):
            for copy in ffn_weights(at, at):
                copy.start()

        halo.wait_recv()
        r.ext[0:16, :] = (r.halo_in[...].astype(F32) * jnp.where(z > 0, 1.0, 0.0)).astype(BF16)

        def lags_at(cols):
            wide = r.ext[:, cols].astype(F32)
            return [wide[16 - lag : 16 - lag + tokens] for lag in range(3)]

        def mix(cols):
            lags = lags_at(cols)
            short = r.short[:, cols].astype(F32)
            return lags, short[0:1] * lags[0] + short[1:2] * lags[1] + short[2:3] * lags[2]

        def chan_copy(k, src, dst, step, to):
            return remote(src, dst, r.za_s.at[k, step - 1], r.za_r.at[k, step - 1], seq=to)

        def to_channels(k, value_ref, make_cols):
            for step in list(range(1, blocks)) + [0]:
                block = block_at(step)
                make_cols(block)
                if step:
                    src, dst = value_ref.at[:, span(block, own)], r.chan.at[span(z, tokens)]
                    send(("za", k), chan_copy(k, src, dst, step, block))
                else:
                    r.chan[span(z, tokens), :] = value_ref[:, span(block, own)]

        def wait_channels(k):
            for step in range(1, blocks):
                source = block_at(blocks - step)
                dst = r.chan.at[span(source, tokens)]
                chan_copy(k, dst, dst, step, source).wait_recv()

        def signal_block(block):
            def body(at):
                base = block * own + at
                cols = pl.ds(pl.multiple_of(base, 128), 128)
                gate_in = mix(pl.ds(pl.multiple_of(width + base, 128), 128))[1]
                values = mix(pl.ds(pl.multiple_of(2 * width + base, 128), 128))[1]
                r.sig[:, cols] = (values * gate_in).astype(BF16)

            tiles(128, own, body)

        to_channels(0, r.sig, signal_block)

        def gate_cols(at):
            cols = pl.ds(at, 128)
            r.gate_out[:, cols] = mix(cols)[1]

        tiles(128, width, gate_cols)

        load_w3.wait()
        load_fade.wait()

        def fading(at):
            lag = (lax.broadcasted_iota(jnp.int32, (tokens, own), 0) + at).astype(F32)
            return jnp.exp(-r.fade[...] * lag)

        def taps_rows(at):
            rows = pl.ds(at, tokens)
            h1, r.s1[:, rows] = sin_cos(mm_tn(r.filt_w1[...], r.features_t[:, rows], precision=HIGHEST))
            h2, r.s2[:, rows] = sin_cos(mm_tn(r.filt_w2[...], h1, precision=HIGHEST))
            r.h1[:, rows] = h1
            r.h2[:, rows] = h2
            taps = mm_tn(h2, r.w3[...], precision=HIGHEST) * fading(at)
            r.qre[rows, :] = taps.astype(BF16)

        tiles(tokens, length, taps_rows)
        load_cs.wait()
        load_sn.wait()
        scale = 1.0 / length

        def taps_spec(at):
            rows = pl.ds(at, tokens)
            real = mm(r.cs[rows, :], r.qre[...]) * scale
            imag = mm(r.sn[rows, :], r.qre[...]) * -scale
            turn_re, turn_im = r.phase[rows, 0:1], r.phase[rows, 1:2]
            r.hre[rows, :] = real * turn_re - imag * turn_im
            r.him[rows, :] = real * turn_im + imag * turn_re

        tiles(tokens, length, taps_spec)
        gather_forward(0)

        wait_channels(0)

        def conv_spec(at):
            rows = pl.ds(at, tokens)
            real = mm(r.cs[rows, :], r.chan[...])
            imag = -mm(r.sn[rows, :], r.chan[...])
            r.xre[rows, :] = real
            r.xim[rows, :] = imag
            hre, him = r.hre[rows, :], r.him[rows, :]
            r.yre[rows, :] = (hre * real - him * imag).astype(BF16)
            r.yim[rows, :] = (-(hre * imag + him * real)).astype(BF16)

        tiles(tokens, length, conv_spec)

        def to_tokens(k):
            for step in list(range(1, blocks)) + [0]:
                block = block_at(step)
                rows = span(block, tokens)
                tile = (mm(r.cs[rows, :], r.yre[...]) + mm(r.sn[rows, :], r.yim[...])).astype(BF16)
                if step:
                    r.conv_out[rows, :] = tile
                    src, dst = r.conv_out.at[rows], r.conv_in.at[z]
                    send(("za", k), chan_copy(k, src, dst, step, block))
                else:
                    r.conv_in[z] = tile

        def wait_tokens(k):
            for step in range(1, blocks):
                source = block_at(blocks - step)
                dst = r.conv_in.at[source]
                chan_copy(k, dst, dst, step, source).wait_recv()

        to_tokens(1)
        gather_forward(1)
        load_wout.wait()
        wait_tokens(1)

        def conv_cols(at):
            return r.conv_in[
                lax.div(at, own), :, pl.ds(pl.multiple_of(lax.rem(at, own), 128), 128)
            ].astype(F32)

        def long_cols(at):
            cols = pl.ds(at, 128)
            long = conv_cols(at) + r.bias[:, cols] * r.sig[:, cols].astype(F32)
            r.long[:, cols] = long
            r.half[:, cols] = (long * r.gate_out[:, cols]).astype(BF16)

        tiles(128, width, long_cols)
        r.res[...] = mm(r.half[...], r.wout[...])
        turned_by_core(r.half, r.gated_turn)
        mine = span(core, tokens)
        pair_rows = chips * share

        def pair_copy(k, src, dst):
            return remote(src, dst, r.cx_s.at[k], r.cx_r.at[k], batch=sibling)

        gated_copy = pair_copy(
            0, r.gated_turn.at[span(1 - core, pair_rows)], r.gated_pair.at[:, mine]
        )
        send("pair", gated_copy)
        r.gated_pair[:, mine] = r.gated_turn[span(core, pair_rows), :]

        def norm2(at):
            rows = pl.ds(at, 32)
            residual = r.res[rows, :] + r.tok[rows, :].astype(F32)
            r.res[rows, :] = residual
            xhat, inverse = norm_parts(residual)
            r.xhat2[rows, :] = xhat
            r.inv2[rows, :] = jnp.broadcast_to(inverse, (32, 128))
            r.half[rows, :] = (xhat * r.gain2[...]).astype(BF16)

        tiles(32, tokens, norm2)
        drain(("ag", 1))
        gather_local(1, r.turn).wait()
        turned(r.half, r.turn)
        gather_start(2, r.turn)
        r.gn2[...] = jnp.zeros((tokens, width), F32)

        def plane_copy(k, src, dst, at, to):
            return remote(src, dst, r.pa_s.at[k, at], r.pa_r.at[k, at], batch=to)

        def chunk_copies(at, to):
            return (
                plane_copy(0, r.hid_send.at[at], r.hid_own.at[:, span(b, tokens)], at, to),
                plane_copy(1, r.pre_send.at[at], r.pre_own.at[span(b, tokens)], at, to),
            )

        def chunk(at, carry):
            slot = lax.rem(at, 2)
            where = span(slot, ffc)
            for copy in ffn_weights(at, slot):
                copy.wait()
            r.gmix[0:tokens, 0:ffc] = mm(r.half[...], r.win[0, :, where])
            r.gmix[0:tokens, ffc : 2 * ffc] = mm_nt(r.cotv[...], r.win[1, where, :])

            def act(row):
                rows = pl.ds(row, 64)
                pre = r.gmix[rows, 0:ffc]
                square = pre * pre
                bent = jnp.tanh(pre * (GELU_SCALE + GELU_SCALE * GELU_CUBIC * square))
                upper = 0.5 + 0.5 * bent
                slope = upper + pre * (0.5 - 0.5 * bent * bent) * (
                    GELU_SCALE + 3.0 * GELU_SCALE * GELU_CUBIC * square
                )
                r.hid_buf[rows, :] = (pre * upper).astype(BF16)
                r.pre_send[at, rows, :] = (r.gmix[rows, ffc : 2 * ffc] * slope).astype(BF16)

            tiles(64, tokens, act)
            r.hid_send[at] = r.hid_buf[...].T

            @pl.when(at < groups - 1)
            def _():
                for copy in chunk_copies(at, lax.rem(b + 1 + at, groups)):
                    copy.start()

            r.res[...] += mm(r.hid_buf[...], r.win[1, where, :])
            r.gn2[...] += mm_nt(r.pre_send[at], r.win[0, :, where])

            @pl.when(at < groups - 2)
            def _():
                for copy in ffn_weights(at + 2, slot):
                    copy.start()

            return carry

        lax.fori_loop(0, groups, chunk, 0)
        for at in range(peers):
            sent.setdefault("ffn", []).extend(chunk_copies(at, group_at(1 + at)))

        def pool_cot():
            return [load(r.win_sem.at[half], r.cot_land.at[half], r.win.at[half]) for half in range(2)]

        def pool_turned(land):
            return [
                load(
                    r.pool_sem.at[at],
                    land.at[at],
                    r.win.at[at // chips, :, pl.ds(at % chips * tokens, tokens)],
                )
                for at in range(groups)
            ]

        gather_local(0, r.cotv).wait()
        gather_finish(0)
        pool = pool_cot()
        r.hid_own[:, span(b, tokens)] = r.hid_send[groups - 1]
        r.pre_own[span(b, tokens), :] = r.pre_send[groups - 1]

        def norm2_back(at, total):
            rows = pl.ds(pl.multiple_of(at * 32, 32), 32)
            r.half[rows, :] = r.res[rows, :].astype(BF16)
            grad, xhat = r.gn2[rows, :], r.xhat2[rows, :]
            back = r.cotv[rows, :].astype(F32) + norm_back(grad, r.gain2[...], xhat, r.inv2[rows, 0:1])
            r.gres[rows, :] = back
            r.gbr_pair[pl.ds(pl.multiple_of(core * tokens + at * 32, 32), 32), :] = back.astype(BF16)
            return total + jnp.sum((grad * xhat).reshape(4, 8, width), axis=0)

        total = lax.fori_loop(0, tokens // 32, norm2_back, jnp.zeros((8, width), F32))
        r.sum_gain2[...] = jnp.sum(total, axis=0, keepdims=True)
        store_layer = load(r.local_sem.at[8], r.half, r.layer_out)
        branch_copy = pair_copy(1, r.gbr_pair.at[mine], r.gbr_pair.at[mine])
        send("pair", branch_copy)

        def gated_back(block):
            cols = span(block, own)
            grad = mm_nt(r.gbr_pair[mine, :], r.wout[span(block, own), :])
            glong = (grad * r.gate_out[:, cols]).astype(BF16)
            r.glong[:, cols] = glong
            r.gmix[0:tokens, cols] = grad * r.long[:, cols]
            r.sum_bias[:, cols] = jnp.sum(
                glong.astype(F32) * r.sig[:, cols].astype(F32), axis=0, keepdims=True
            )

        to_channels(2, r.glong, gated_back)

        branch_copy.wait_recv()
        gated_copy.wait_recv()
        for step in list(range(1, chips)) + [0]:
            to = lax.rem(chip + step, chips)
            part = mm(r.gated_pair[span(to, share), :], r.gbr_pair[...])
            if step:
                at = step - 1
                r.out_send[at] = part.astype(BF16)
                sems = r.wo_s.at[0, at], r.wo_r.at[0, at]
                send("out", remote(r.out_send.at[at], r.out_land.at[at], *sems, batch=to * 2 + core))
            else:
                r.out_own[...] = part
        gather_forward(2)

        near = z + 1 - 2 * lax.rem(z, 2)
        far = block_at(2)

        def reduce_first(k, refs):
            return remote(refs[0], refs[1], r.rs_s.at[k, 0], r.rs_r.at[k, 0], seq=near)

        def reduce_second(k, refs):
            return remote(refs[2], refs[3], r.rs_s.at[k, 1], r.rs_r.at[k, 1], seq=far)

        def reduce_send(k, refs, part_of):
            send_ref, _, next_ref, _, own_ref = refs
            send_ref[0] = part_of(near).astype(BF16)
            send_ref[1] = part_of(lax.rem(near + 2, blocks)).astype(BF16)
            send("rs", reduce_first(k, refs))
            next_ref[...] = part_of(far).astype(BF16)
            own_ref[...] = part_of(z)

        def reduce_next(k, refs):
            _, land_ref, next_ref, _, own_ref = refs
            reduce_first(k, refs).wait_recv()
            next_ref[...] = (next_ref[...].astype(F32) + land_ref[1].astype(F32)).astype(BF16)
            send("rs", reduce_second(k, refs))
            own_ref[...] += land_ref[0].astype(F32)

        def reduce_finish(k, refs):
            reduce_second(k, refs).wait_recv()
            refs[4][...] += refs[3][...].astype(F32)

        down_refs = (r.down_send, r.down_land, r.down_next, r.down_last, r.down_own)
        up_refs = (r.up_send, r.up_land, r.up_next, r.up_last, r.up_own)
        in_refs = (r.in_send, r.in_land, r.in_next, r.in_last, r.in_own)

        def wait_plane(k, dst_of):
            for at in range(peers):
                source = group_at(groups - 1 - at)
                dst = dst_of(source)
                plane_copy(k, dst, dst, at, source).wait_recv()

        deep = groups // 2 * tokens

        def down_part(block):
            rows = span(block, ffc // blocks)
            return mm(r.hid_own[rows, :deep], r.win[0]) + mm(r.hid_own[rows, deep:], r.win[1])

        def turned_part(right_ref):
            def part(block):
                rows = span(block, own)
                return mm(r.win[0, rows, :], right_ref[:deep]) + mm(r.win[1, rows, :], right_ref[deep:])

            return part


        wait_channels(2)

        def grad_spec(at):
            rows = pl.ds(at, tokens)
            real = mm(r.cs[rows, :], r.chan[...])
            imag = -mm(r.sn[rows, :], r.chan[...])
            hre, him = r.hre[rows, :], r.him[rows, :]
            r.yre[rows, :] = (hre * real + him * imag).astype(BF16)
            r.yim[rows, :] = (him * real - hre * imag).astype(BF16)
            xre, xim = r.xre[rows, :], r.xim[rows, :]
            both_re = xre * real + xim * imag
            both_im = xre * imag - xim * real
            turn_re, turn_im = r.phase[rows, 0:1], r.phase[rows, 1:2]
            r.qre[rows, :] = ((both_re * turn_re + both_im * turn_im) * scale).astype(BF16)
            r.qim[rows, :] = ((both_re * turn_im - both_im * turn_re) * scale).astype(BF16)

        tiles(tokens, length, grad_spec)
        drain(("za", 1))
        to_tokens(3)
        r.w12[...] = jnp.zeros((net_rows, 128), F32)
        r.sum_w3[...] = jnp.zeros((filt, own), F32)
        for at in range(0, length, tokens):
            rows = slice(at, at + tokens)
            grad_taps = mm(r.cs[rows, :], r.qre[...]) + mm(r.sn[rows, :], r.qim[...])
            grad_filt = grad_taps * fading(at)
            r.sum_w3[...] += mm(r.h2[:, rows], grad_filt, precision=HIGHEST)
            grad_angle2 = mm_nt(r.w3[...], grad_filt, precision=HIGHEST) * r.s2[:, rows]
            r.w12[net_at:, :filt] += mm_nt(r.h1[:, rows], grad_angle2, precision=HIGHEST)
            grad_angle1 = mm(r.filt_w2[...], grad_angle2, precision=HIGHEST) * r.s1[:, rows]
            r.w12[:emb, :filt] += mm_nt(r.features_t[:, rows], grad_angle1, precision=HIGHEST)

        def small_copy(k, src, dst, at, to):
            return remote(src, dst, r.sm_s.at[k, at], r.sm_r.at[k, at], batch=to)

        def small_z_copy(k, src, dst, step, to):
            return remote(src, dst, r.sz_s.at[k, step - 1], r.sz_r.at[k, step - 1], seq=to)

        def small_z_send(k, src, dst_of):
            for step in range(1, blocks):
                send("small", small_z_copy(k, src, dst_of(step), step, block_at(step)))

        def small_z_wait(k, dst_of):
            for step in range(1, blocks):
                dst = dst_of(step)
                small_z_copy(k, dst, dst, step, block_at(blocks - step)).wait_recv()

        def small_send(k, src_of, dst_of):
            for at in range(peers):
                to = group_at(1 + at)
                send("small", small_copy(k, src_of(to), dst_of(at), at, to))

        def small_wait(k, dst_of):
            for at in range(peers):
                dst = dst_of(at)
                small_copy(k, dst, dst, at, group_at(groups - 1 - at)).wait_recv()

        w3_rows = filt // groups
        small_z_send(0, r.w12, lambda step: r.w12_z.at[step - 1])
        small_send(0, lambda to: r.sum_w3.at[span(to, w3_rows)], lambda at: r.w3_land.at[at])

        def outz_copy(step, to):
            sems = r.wo_s.at[1, step - 1], r.wo_r.at[1, step - 1]
            return remote(r.outz_send.at[span(to, rows_out)], r.outz_land.at[step - 1], *sems, seq=to)

        for step in range(1, chips):
            land = r.out_land.at[step - 1]
            sems = r.wo_s.at[0, step - 1], r.wo_r.at[0, step - 1]
            source = lax.rem(chip + chips - step, chips) * 2 + core
            remote(land, land, *sems, batch=source).wait_recv()
        total = r.out_own[...]
        for step in range(chips - 1):
            total = total + r.out_land[step].astype(F32)
        r.out_own[...] = total
        r.outz_send[...] = total.astype(BF16)
        for step in range(1, blocks):
            send("outz", outz_copy(step, block_at(step)))
        r.outz_own[...] = r.out_own[span(z, rows_out), :]

        wait_tokens(3)

        def short_sums(cols, grad, lags):
            for lag in range(3):
                r.sum_short[lag : lag + 1, cols] = jnp.sum(grad * lags[lag], axis=0, keepdims=True)

        def mixed_cols(at):
            cols = pl.ds(at, 128)
            grad_signal = conv_cols(at) + r.bias[:, cols] * r.glong[:, cols].astype(F32)
            gate_cols = pl.ds(pl.multiple_of(width + at, 128), 128)
            value_cols = pl.ds(pl.multiple_of(2 * width + at, 128), 128)
            gate_lags, gate_in = mix(gate_cols)
            value_lags, values = mix(value_cols)
            grad_gate = grad_signal * values
            r.gmix[0:tokens, gate_cols] = grad_gate
            short_sums(gate_cols, grad_gate, gate_lags)
            grad_value = grad_signal * gate_in
            r.gmix[0:tokens, value_cols] = grad_value
            short_sums(value_cols, grad_value, value_lags)

        tiles(128, width, mixed_cols)
        halo = remote(
            r.gmix.at[0:8], r.gmix.at[tokens : tokens + 8],
            r.halo_s.at[1], r.halo_r.at[1], seq=block_at(blocks - 1),
        )
        send("halo", halo)

        def gate_short(at):
            cols = pl.ds(at, 128)
            short_sums(cols, r.gmix[0:tokens, cols], lags_at(cols))

        tiles(128, width, gate_short)
        small_z_wait(0, lambda step: r.w12_z.at[step - 1])
        net = r.w12[...]
        for step in range(zpeers):
            net = net + r.w12_z[step]
        r.w12_sum[...] = net
        small_send(1, lambda to: r.w12_sum, lambda at: r.w12_plane.at[at])
        small_wait(0, lambda at: r.w3_land.at[at])
        part = r.sum_w3[span(b, w3_rows), :]
        for at in range(peers):
            part = part + r.w3_land[at]
        r.w3_part[...] = part
        r.w3_all[z, span(b, w3_rows), :] = part
        small_send(2, lambda to: r.w3_part, lambda at: r.w3_all.at[z, span(b, w3_rows)])
        halo.wait_recv()
        r.gmix[tokens:, :] = r.gmix[tokens:, :] * jnp.where(z < blocks - 1, 1.0, 0.0)

        drain(("forward", 0))
        for step in list(range(1, groups)) + [0]:
            group = group_at(step)

            def proj_cols(at, group=group):
                cols = pl.ds(pl.multiple_of(group * inc + at, 128), 128)
                short = r.short[:, cols].astype(F32)
                grads = [r.gmix[lag : lag + tokens, cols] for lag in range(3)]
                total = short[0:1] * grads[0] + short[1:2] * grads[1] + short[2:3] * grads[2]
                r.gproj[:, cols] = total.astype(BF16)

            tiles(128, inc, proj_cols)
            mine = r.gproj_own.at[span(b, tokens)]
            if step:
                send("gproj", plane_copy(2, r.gproj.at[:, span(group, inc)], mine, step - 1, group))
            else:
                r.gproj_own[span(b, tokens), :] = r.gproj[:, span(group, inc)]

        def spread(k, own_ref, out_ref, size):
            for at in range(peers):
                to = group_at(1 + at)
                src, dst = own_ref.at[span(to, rows_out)], out_ref.at[:, span(b, size)]
                send("spread", remote(src, dst, r.tr_s.at[k, at], r.tr_r.at[k, at], batch=to))
            return load(r.local_sem.at[14 + k], own_ref.at[span(b, rows_out)], out_ref.at[:, span(b, size)])

        def spread_finish(k, copy, out_ref, size):
            for at in range(peers):
                source = group_at(groups - 1 - at)
                dst = out_ref.at[:, span(source, size)]
                remote(dst, dst, r.tr_s.at[k, at], r.tr_r.at[k, at], batch=source).wait_recv()
            copy.wait()

        for copy in pool:
            copy.wait()
        wait_plane(0, lambda at: r.hid_own.at[:, span(at, tokens)])
        reduce_send(0, down_refs, down_part)
        gather_local(2, r.turn).wait()
        gather_finish(2)
        pool = pool_turned(r.n2_land)
        small_wait(1, lambda at: r.w12_plane.at[at])
        net = r.w12_sum[...]
        for at in range(peers):
            net = net + r.w12_plane[at]
        r.grad_w1[...] = net[:emb, :filt]
        r.grad_w2[...] = net[net_at:, :filt]
        for at in range(peers):
            dst = r.w3_all.at[z, span(group_at(groups - 1 - at), w3_rows)]
            small_copy(2, dst, dst, at, group_at(groups - 1 - at)).wait_recv()
        small_z_send(1, r.w3_all.at[z], lambda step: r.w3_all.at[z])
        for copy in pool:
            copy.wait()
        wait_plane(1, lambda at: r.pre_own.at[span(at, tokens)])
        reduce_next(0, down_refs)
        reduce_send(1, up_refs, turned_part(r.pre_own))
        win_loads = [(block, load_win(block)) for block in range(2)]
        for step in range(1, blocks):
            outz_copy(step, block_at(blocks - step)).wait_recv()
        total = r.outz_own[...]
        for step in range(zpeers):
            total = total + r.outz_land[step].astype(F32)
        r.outz_own[...] = total
        store_out = load(r.local_sem.at[11], r.outz_own, r.grad_w_out)
        reduce_finish(0, down_refs)
        store_down = load(r.local_sem.at[9], r.down_own, r.grad_w_down)
        for _, copy in win_loads:
            copy.wait()
        r.gn2[...] = mm_nt(r.gproj[:, :width], r.win[0])
        r.gn2[...] += mm_nt(r.gproj[:, width : 2 * width], r.win[1])
        reduce_next(1, up_refs)
        gather_finish(1)
        pool = pool_turned(r.n1_land)
        r.gn2[...] += mm_nt(r.gproj[:, 2 * width :], r.win[2])

        def norm1_back(at, total):
            rows = pl.ds(pl.multiple_of(at * 32, 32), 32)
            grad, inverse = r.gn2[rows, :], r.inv1[rows, 0:1]
            xhat = (r.tok[rows, :].astype(F32) - r.mean1[rows, 0:1]) * inverse
            r.res[rows, :] = r.gres[rows, :] + norm_back(grad, r.gain1[...], xhat, inverse)
            return total + jnp.sum((grad * xhat).reshape(4, 8, width), axis=0)

        total = lax.fori_loop(0, tokens // 32, norm1_back, jnp.zeros((8, width), F32))
        r.sum_gain1[...] = jnp.sum(total, axis=0, keepdims=True)
        r.small_send[...] = jnp.zeros((groups, 16, share), F32)
        for group in range(groups):
            cols = slice(group * share, (group + 1) * share)
            r.small_send[group, 0:1, :] = r.sum_gain1[:, cols]
            r.small_send[group, 1:2, :] = r.sum_gain2[:, cols]
            r.small_send[group, 2:3, :] = r.sum_bias[:, cols]
            for lag in range(3):
                for third in range(3):
                    at = group * inc + third * share
                    row = 3 + 3 * lag + third
                    r.small_send[group, row : row + 1, :] = r.sum_short[lag : lag + 1, at : at + share]
        small_send(3, lambda to: r.small_send.at[to], lambda at: r.small_land.at[b])
        r.small_land[b] = r.small_send[b]
        store_tokens = load(r.local_sem.at[13], r.res, r.tokens_grad)
        for copy in pool:
            copy.wait()
        wait_plane(2, lambda at: r.gproj_own.at[span(at, tokens)])
        reduce_send(2, in_refs, turned_part(r.gproj_own))
        reduce_finish(1, up_refs)
        spread_up = spread(0, r.up_own, r.grad_w_up, ffc)
        for at in range(peers):
            source = group_at(groups - 1 - at)
            dst = r.small_land.at[source]
            small_copy(3, dst, dst, at, source).wait_recv()
        small = r.small_land[0]
        for group in range(1, groups):
            small = small + r.small_land[group]
        r.small_sum[...] = small
        small_z_send(2, r.small_sum, lambda step: r.small_z.at[step - 1])
        reduce_next(2, in_refs)
        reduce_finish(2, in_refs)
        spread_in = spread(1, r.in_own, r.grad_w_in, inc)

        def chosen(value, size):
            picked = value[:, :size]
            for block in range(1, blocks):
                picked = jnp.where(z == block, value[:, block * size : (block + 1) * size], picked)
            return picked

        for step in range(1, blocks):
            source = block_at(blocks - step)
            dst = r.w3_all.at[source]
            small_z_copy(1, dst, dst, step, source).wait_recv()
        third = r.w3_all[lax.div(b * share, own)]
        halves = own // share
        picked = third[:, :share]
        for half in range(1, halves):
            here = lax.rem(b, halves) == half
            picked = jnp.where(here, third[:, half * share : (half + 1) * share], picked)
        r.grad_w3[...] = chosen(picked, rows_out)
        small_z_wait(2, lambda step: r.small_z.at[step - 1])
        small = r.small_sum[...]
        for step in range(zpeers):
            small = small + r.small_z[step]
        r.grad_gain1[...] = chosen(small[0:1], rows_out)
        r.grad_gain2[...] = chosen(small[1:2], rows_out)
        r.grad_bias[...] = chosen(small[2:3], rows_out)
        for lag in range(3):
            for third in range(3):
                row = 3 + 3 * lag + third
                r.short_all[lag : lag + 1, third * share : (third + 1) * share] = small[row : row + 1]
        r.grad_short[...] = chosen(r.short_all[0:3, :], 3 * rows_out)
        spread_finish(0, spread_up, r.grad_w_up, ffc)
        spread_finish(1, spread_in, r.grad_w_in, inc)
        store_layer.wait()
        store_down.wait()
        store_out.wait()
        store_tokens.wait()
        for key in list(sent):
            drain(key)

    def call(args):
        result = pl.pallas_call(
            kernel,
            out_shape=[jax.ShapeDtypeStruct(shape, dtype) for shape, dtype, _ in outputs.values()],
            in_specs=[pl.BlockSpec(memory_space=space) for space in inputs.values()],
            out_specs=[pl.BlockSpec(memory_space=space) for *_, space in outputs.values()],
            scratch_shapes=list(scratch.values()),
            compiler_params=pltpu.CompilerParams(
                collective_id=0, has_side_effects=True, vmem_limit_bytes=KERNEL_VMEM
            ),
        )(*[args[name] for name in inputs])
        return settled(result[:13])

    return call


def settled(values):
    count = len(values)

    def copy_all(*refs):
        for source, target in zip(refs[:count], refs[count:]):
            target[...] = source[...].reshape(target.shape)

    return pl.pallas_call(
        copy_all,
        out_shape=[
            jax.ShapeDtypeStruct(value.shape[1:] if value.shape[0] == 1 else value.shape, value.dtype)
            for value in values
        ],
        in_specs=[pl.BlockSpec(memory_space=pltpu.VMEM)] * count,
        out_specs=[pl.BlockSpec(memory_space=pltpu.VMEM)] * count,
    )(*values)


def small_sums(gain1, bias, gain2, short, w1, w2, w3_own):
    blocks, position = lax.axis_size("seq"), lax.axis_index("seq")
    dests = lax.axis_size("batch") * blocks
    width, (filt_dim, own), emb = gain1.shape[0], w3_own.shape, w1.shape[0]
    w3_all = lax.dynamic_update_slice_in_dim(
        jnp.zeros((filt_dim, width), F32), w3_own, position * own, 1
    )
    share = width // dests
    small = jnp.concatenate(
        [
            gain1.reshape(dests, share),
            bias.reshape(dests, share),
            gain2.reshape(dests, share),
            short.reshape(3, dests, 3 * share).transpose(1, 0, 2).reshape(dests, 9 * share),
            w3_all.reshape(filt_dim, dests, share).transpose(1, 0, 2).reshape(dests, filt_dim * share),
        ],
        axis=1,
    )
    small = scatter_sum(small, wire=F32)[0]
    filters = all_sum(jnp.concatenate([w1, w2], axis=0))
    return (
        small[:share],
        small[3 * share : 12 * share].reshape(3, 3 * share),
        filters[:emb],
        filters[emb:],
        small[12 * share :].reshape(filt_dim, share),
        small[share : 2 * share],
        small[2 * share : 3 * share],
    )


def kernel_layer(
    tokens,
    norm_gain1,
    w_in,
    short_kernel,
    filt_w1,
    filt_w2,
    filt_w3,
    decay_rate,
    conv_bias,
    w_out,
    norm_gain2,
    w_up,
    w_down,
    cotangent,
):
    _, block_len, width = tokens.shape
    groups, blocks = lax.axis_size("batch"), lax.axis_size("seq")
    emb, filt = filt_w1.shape
    (cosine, sine), phase = symmetric_tables(block_len * blocks)
    features = lag_features(emb, block_len * blocks)
    call = kernel_plan(groups, blocks, block_len, width, w_up.shape[1], filt, emb)
    out = call(
        dict(
            tokens=tokens[0],
            cot=cotangent[0],
            w_in=w_in,
            w_out=w_out,
            w_up=w_up,
            w_down=w_down,
            cosine=jnp.asarray(cosine),
            sine=jnp.asarray(sine),
            filt_w3=filt_w3,
            decay=decay_rate[None],
            gain1=norm_gain1[None],
            gain2=norm_gain2[None],
            bias=conv_bias[None],
            short=short_kernel,
            filt_w1=filt_w1,
            filt_w2=filt_w2,
            features_t=jnp.asarray(features.T),
            phase=jnp.asarray(phase),
        )
    )
    layer_out, tokens_grad, w_in, w_out, w_up, w_down, gain1, gain2, bias, short, w1, w2, w3 = out
    return layer_out[None], tokens_grad[None], (gain1, short, w1, w2, w3, bias, gain2), (w_in, w_out, w_up, w_down)


def on_device(*args):
    tokens = args[0]
    fits = lax.axis_size("batch") == 8 and lax.axis_size("seq") == 4 and tokens.shape[1] * lax.axis_size("seq") <= 1024
    layer = kernel_layer if fits else plain_layer
    layer_out, tokens_grad, small, large = layer(*args)
    gain1, short, w1, w2, w3, bias, gain2 = small
    grad_w_in, grad_w_out, grad_w_up, grad_w_down = large
    return (
        layer_out, tokens_grad, gain1, grad_w_in, short, w1, w2, w3, bias, grad_w_out, gain2,
        grad_w_up, grad_w_down,
    )


def solution(mesh):
    split = P("batch", "seq", None)
    both = ("batch", "seq")
    return jax.shard_map(
        on_device,
        mesh=mesh,
        in_specs=(split,) + (P(),) * 12 + (split,),
        out_specs=(
            split,
            split,
            P(both),
            P(both, None),
            P(None, both),
            P(),
            P(),
            P(None, both),
            P(both),
            P(both, None),
            P(both),
            P(both, None),
            P(both, None),
        ),
        check_vma=False,
    )
```

time: 1570 us -> 225 us (0.14)
  waiting for transfers between devices: 1160 us -> 0 us
  Pallas kernels: 0 us -> 222 us
  matrix products: 185 us -> 0 us
  other arithmetic: 80.2 us -> 0 us
  local copies, waits for them, and re-layouts: 74 us -> 1.44 us
  blocking collectives: 41.9 us -> 0 us
    reduce_scatter x5 -> x0, waiting for transfers between devices: 1160 us -> none  [the longest x1 366 us: on_device(): lax.psum_scatter(grad_up, ('batch', 'seq'), scatter_dimension=0, tiled=True)]
    pallas_call x0 -> x2, Pallas kernels: none -> 222 us  [the longest x1 219 us: call(): pl.pallas_call(kernel, out_shape=[jax.ShapeDtypeStruct(shape, dtype) for...]
    dot_general x43 -> x0, matrix products: 185 us -> none  [the longest x1 32 us: on_device(): jnp.einsum('nf,kfd->knd', inverse_table, grad_filter_spec, precision=high...]
    unnamed x1 -> x0, blocking collectives: 41.9 us -> none
    unnamed x219 -> x1, local copies, waits for them, and re-layouts: 36.6 us -> 1.44 us
    dynamic_slice x1 -> x0, local copies, waits for them, and re-layouts: 29 us -> none  [filter_at(): lax.dynamic_index_in_dim(filter_spec, jnp.clip(lag_steps, 0, blocks - 1),...]
    dynamic_update_slice x4 -> x0, other arithmetic: 21.1 us -> none  [on_device(): lax.dynamic_update_index_in_dim(grad_filter, current + jnp.where(lag_filt...]
    add x6 -> x0, other arithmetic: 21 us -> none  [the longest x2 14.2 us: spec_conj_mul(): left_re * right_re + left_im * right_im]
  transfers between devices with their start and end apart: 10 -> 0, of which waited for: 6 -> 0; matrix products, arithmetic and copies ran while one was open for 14% -> 0% of each run, Pallas kernels for 0% -> 0%
where the time goes in v1:
time: 225 us; the launch traced here: 224 us
  Pallas kernels  222 us (99%)
    pallas_call x1, Pallas kernels, call(): pl.pallas_call(kernel, out_shape=[jax.ShapeDtypeStruct(shape, dtype) for...  219 us

profile of v1, /device:TPU:1, one launch (start us, length us, event | category | flops | bytes accessed | tf_op | source)
XLA Modules:
  0.0 224.3 jit_solution(15413104949775955253)
XLA Ops:
  0.7 218.6 %shard_map.273 = (bf16[256,1024]{1,0:T(8,128)(2,1)}, f32[256,1024]{1,0:T(8,128)}, f32[32,3072]{1,0:T(8,128)}, f32[32,1024]{1,0:T(8,128)}, f32[32,4096]{1,0:T(8,1...) custom-call(bf16[256,1024]{1,0:T(8,128)(2,1)} %bitcast.8, ...), custom_call_target="tpu_custom_call" | custom-call | tf_op jit(solution)/shard_map/pallas_call | solution.py:1191
  219.3 3.6 %shard_map.274 = (bf16[256,1024]{1,0:T(8,128)(2,1)}, f32[256,1024]{1,0:T(8,128)}, f32[32,3072]{1,0:T(8,128)}, f32[32,1024]{1,0:T(8,128)}, f32[32,4096]{1,0:T(8,1...) custom-call(bf16[256,1024]{1,0:T(8,128)(2,1)} %get-tuple-element.39., ...), custom_call_target="tpu_custom_call" | custom-call | tf_op jit(solution)/shard_map/pallas_call | solution.py:1213
  222.9 1.4 copy.31

commit v2 on v1

--- a/solution.py
+++ b/solution.py
@@ -324,6 +324,7 @@
     share = width // groups
     rows_out = share // blocks
     inc = 3 * share
+    spare = 16
     chips = groups // 2
     down_rows = ffc // blocks
     net_at = -(-emb // 8) * 8
@@ -351,22 +352,25 @@
         grad_w2=((filt, filt), F32, vm),
         grad_w3=((filt, rows_out), F32, vm),
         cot_land=((2, groups // 2 * tokens, width), BF16, hbm),
-        n1_land=((groups, width, tokens), BF16, hbm),
         n2_land=((groups, width, tokens), BF16, hbm),
     )
     dma = pltpu.SemaphoreType.DMA
     scratch = dict(
         tok=vm((tokens, width), BF16), cotv=vm((tokens, width), BF16),
         mean1=vm((tokens, 128), F32), inv1=vm((tokens, 128), F32),
-        n1=vm((tokens, width), BF16), turn=vm((width, tokens), BF16),
+        n1_all=vm((length, width), BF16), turn=vm((width, tokens), BF16),
         gated_turn=vm((width, tokens), BF16), gated_pair=vm((width // 2, 2 * tokens), BF16),
-        hid_buf=vm((tokens, ffc), BF16), gmix=vm((tokens + 8, 3 * width), F32),
+        hid_buf=vm((tokens, ffc), BF16),
+        ghalo=vm((8, 3 * width), F32), ghalo_in=vm((8, 3 * width), F32), tail=vm((16, 3 * width), F32),
+        ext_c=vm((length + 32, 3 * own), BF16), gproj_c=vm((length, 3 * own), BF16),
+        gconv_c=vm((length + 16, own), BF16), glong_c=vm((length + 16, own), BF16),
+        ggb=vm((tokens, width), BF16),
         win=vm((3, width, width), BF16), wout=vm((width, width), BF16),
         cs=vm((length, length), BF16), sn=vm((length, length), BF16),
         ext=vm((tokens + 16, 3 * width), BF16),
         halo_out=vm((16, 3 * width), BF16), halo_in=vm((16, 3 * width), BF16),
         gate_out=vm((tokens, width), F32),
-        sig=vm((tokens, width), BF16), chan=vm((length, own), BF16),
+        sig=vm((tokens, width), BF16), chan=vm((length + 16, own), BF16),
         w3=vm((filt, own), F32), fade=vm((1, own), F32),
         h1=vm((filt, length), F32), s1=vm((filt, length), F32),
         h2=vm((filt, length), F32), s2=vm((filt, length), F32),
@@ -383,7 +387,7 @@
         xre=vm((length, own), F32), xim=vm((length, own), F32),
         yre=vm((length, own), BF16), yim=vm((length, own), BF16),
         qre=vm((length, own), BF16), qim=vm((length, own), BF16),
-        conv_out=vm((length, own), BF16), conv_in=vm((blocks, tokens, own), BF16),
+        conv_out=vm((length + 16, own), BF16), conv_in=vm((blocks, tokens, own), BF16),
         long=vm((tokens, width), F32), half=vm((tokens, width), BF16),
         res=vm((tokens, width), F32), xhat2=vm((tokens, width), F32),
         inv2=vm((tokens, 128), F32), gn2=vm((tokens, width), F32),
@@ -392,16 +396,14 @@
         pre_send=vm((groups, tokens, ffc), BF16), pre_own=vm((groups * tokens, ffc), BF16),
         gbr_pair=vm((2 * tokens, width), BF16),
         glong=vm((tokens, width), BF16),
-        gproj=vm((tokens, 3 * width), BF16), gproj_own=vm((groups * tokens, inc), BF16),
+        gproj=vm((tokens, 3 * width), BF16),
         down_send=vm((2, down_rows, width), BF16), down_land=vm((2, down_rows, width), BF16),
         down_next=vm((down_rows, width), BF16), down_last=vm((down_rows, width), BF16),
-        down_own=vm((down_rows, width), F32),
         up_send=vm((2, own, ffc), BF16), up_land=vm((2, own, ffc), BF16),
-        up_next=vm((own, ffc), BF16), up_last=vm((own, ffc), BF16), up_own=vm((own, ffc), F32),
-        in_send=vm((2, own, inc), BF16), in_land=vm((2, own, inc), BF16),
-        in_next=vm((own, inc), BF16), in_last=vm((own, inc), BF16), in_own=vm((own, inc), F32),
+        up_next=vm((own, ffc), BF16), up_last=vm((own, ffc), BF16),
+        in_send=vm((chips, share, 3 * own), BF16), in_pair=vm((chips, share, 3 * own), BF16),
+        in_land=vm((chips - 1, share, 3 * own), BF16), in_own=vm((share, 3 * own), F32),
         out_send=vm((chips - 1, share, width), BF16), out_land=vm((chips - 1, share, width), BF16),
-        out_own=vm((share, width), F32),
         outz_send=vm((share, width), BF16), outz_land=vm((zpeers, rows_out, width), BF16),
         outz_own=vm((rows_out, width), F32),
         load_sem=dma((16,)),
@@ -409,16 +411,17 @@
         win_sem=dma((3,)),
         ffn_sem=dma((2, 2)),
         local_sem=dma((16,)),
-        stage=vm((chips - 1, width, tokens), BF16), stage_sem=dma((chips - 1,)),
-        ag_s=dma((3, groups - 1)), ag_r=dma((3, groups - 1)),
+        stage_sem=dma((chips - 1,)),
+        ag_s=dma((2, groups - 1)), ag_r=dma((2, groups - 1)),
         halo_s=dma((2,)), halo_r=dma((2,)),
         za_s=dma((4, zpeers)), za_r=dma((4, zpeers)),
-        pa_s=dma((3, peers)), pa_r=dma((3, peers)),
-        cx_s=dma((2,)), cx_r=dma((2,)), wo_s=dma((2, chips - 1)), wo_r=dma((2, chips - 1)),
-        rs_s=dma((3, 2)), rs_r=dma((3, 2)),
+        pa_s=dma((2, peers)), pa_r=dma((2, peers)),
+        cx_s=dma((3,)), cx_r=dma((3,)), zg_s=dma((zpeers,)), zg_r=dma((zpeers,)),
+        wi_s=dma((chips - 1,)), wi_r=dma((chips - 1,)), ti_s=dma((zpeers, 3)), ti_r=dma((zpeers, 3)), wo_s=dma((2, chips - 1)), wo_r=dma((2, chips - 1)),
+        rs_s=dma((2, 2)), rs_r=dma((2, 2)),
         sm_s=dma((4, peers)), sm_r=dma((4, peers)),
         sz_s=dma((3, zpeers)), sz_r=dma((3, zpeers)),
-        tr_s=dma((2, peers)), tr_r=dma((2, peers)),
+        tr_s=dma((1, peers)), tr_r=dma((1, peers)),
     )
     names = [*inputs, *outputs, *scratch]
 
@@ -481,11 +484,9 @@
             pl.semaphore_signal(barrier, inc=1, device_id={"batch": group_at(step)}, device_id_type=MESH)
         for step in range(1, blocks):
             pl.semaphore_signal(barrier, inc=1, device_id={"seq": block_at(step)}, device_id_type=MESH)
-        pl.semaphore_wait(barrier, peers + zpeers)
 
         slots = [
             lambda at: r.cot_land.at[lax.div(at, chips), span(lax.rem(at, chips), tokens)],
-            lambda at: r.n1_land.at[at],
             lambda at: r.n2_land.at[at],
         ]
 
@@ -505,11 +506,9 @@
         def stage(k, step):
             if k == 0:
                 return r.gproj.at[:, (step - 1) * width : step * width]
-            return r.stage.at[step - 1]
+            return r.win.at[0, :, (step - 1) * tokens : step * tokens]
 
         def gather_forward(k):
-            if k >= 2:
-                drain(("forward", k - 1))
             staged = []
             for step in range(1, chips):
                 slot = slots[k](lax.rem(chip + chips - step, chips) * 2 + core)
@@ -544,9 +543,6 @@
 
             tiles(share, width, body)
 
-        load_cot.wait()
-        gather_start(0, r.cotv)
-
         load_tok.wait()
 
         def norm1(at):
@@ -555,35 +551,46 @@
             xhat, inverse = norm_parts(x)
             r.mean1[rows, :] = jnp.broadcast_to(jnp.mean(x, axis=-1, keepdims=True), (32, 128))
             r.inv1[rows, :] = jnp.broadcast_to(inverse, (32, 128))
-            r.n1[rows, :] = (xhat * r.gain1[...]).astype(BF16)
+            r.n1_all[pl.ds(pl.multiple_of(z * tokens + at, 32), 32), :] = (xhat * r.gain1[...]).astype(BF16)
 
         tiles(32, tokens, norm1)
         for block, copy in win_loads:
             copy.wait()
             cols = slice(block * width, (block + 1) * width)
-            proj = mm(r.n1[...], r.win[block], out=BF16)
+            proj = mm(r.n1_all[span(z, tokens), :], r.win[block], out=BF16)
             r.ext[16:, cols] = proj
             r.halo_out[:, cols] = proj[tokens - 16 :]
+        pl.semaphore_wait(barrier, peers + zpeers)
         halo = remote(r.halo_out, r.halo_in, r.halo_s.at[0], r.halo_r.at[0], seq=block_at(1))
         send("halo", halo)
-        turned(r.n1, r.turn)
-        gather_start(1, r.turn)
-
-        def ffn_weights(at, slot):
+        own_loads = [
+            load(
+                r.load_sem.at[7 + part],
+                r.w_in.at[:, pl.ds(pl.multiple_of(part * width + z * own, own), own)],
+                r.win.at[2, :, part * own : (part + 1) * own],
+            )
+            for part in range(3)
+        ]
+        for padded in (r.chan, r.conv_out, r.gconv_c, r.glong_c):
+            padded[length:, :] = jnp.zeros((spare, own), BF16)
+        r.ext_c[0:spare, :] = jnp.zeros((spare, 3 * own), BF16)
+        r.ext_c[length + spare :, :] = jnp.zeros((spare, 3 * own), BF16)
+
+        def up_weights(at, slot):
             group = lax.rem(b + 1 + at, groups)
-            where = span(slot, ffc)
-            return (
-                pltpu.make_async_copy(
-                    r.w_up.at[:, span(group, ffc)], r.win.at[0, :, where], r.ffn_sem.at[slot, 0]
-                ),
-                pltpu.make_async_copy(
-                    r.w_down.at[span(group, ffc)], r.win.at[1, where], r.ffn_sem.at[slot, 1]
-                ),
+            return pltpu.make_async_copy(
+                r.w_up.at[:, span(group, ffc)], r.win.at[0, :, span(slot, ffc)], r.ffn_sem.at[slot, 0]
             )
 
+        def down_weights(at, slot):
+            group = lax.rem(b + 1 + at, groups)
+            return pltpu.make_async_copy(
+                r.w_down.at[span(group, ffc)], r.win.at[1, span(slot, ffc)], r.ffn_sem.at[slot, 1]
+            )
+
         for at in range(2):
-            for copy in ffn_weights(at, at):
-                copy.start()
+            down_weights(at, at).start()
+            up_weights(at, at).start()
 
         halo.wait_recv()
         r.ext[0:16, :] = (r.halo_in[...].astype(F32) * jnp.where(z > 0, 1.0, 0.0)).astype(BF16)
@@ -628,12 +635,6 @@
 
         to_channels(0, r.sig, signal_block)
 
-        def gate_cols(at):
-            cols = pl.ds(at, 128)
-            r.gate_out[:, cols] = mix(cols)[1]
-
-        tiles(128, width, gate_cols)
-
         load_w3.wait()
         load_fade.wait()
 
@@ -664,14 +665,13 @@
             r.him[rows, :] = real * turn_im + imag * turn_re
 
         tiles(tokens, length, taps_spec)
-        gather_forward(0)
 
         wait_channels(0)
 
         def conv_spec(at):
             rows = pl.ds(at, tokens)
-            real = mm(r.cs[rows, :], r.chan[...])
-            imag = -mm(r.sn[rows, :], r.chan[...])
+            real = mm(r.cs[rows, :], r.chan[0:length, :])
+            imag = -mm(r.sn[rows, :], r.chan[0:length, :])
             r.xre[rows, :] = real
             r.xim[rows, :] = imag
             hre, him = r.hre[rows, :], r.him[rows, :]
@@ -680,14 +680,14 @@
 
         tiles(tokens, length, conv_spec)
 
-        def to_tokens(k):
+        def to_tokens(k, out_ref):
             for step in list(range(1, blocks)) + [0]:
                 block = block_at(step)
                 rows = span(block, tokens)
                 tile = (mm(r.cs[rows, :], r.yre[...]) + mm(r.sn[rows, :], r.yim[...])).astype(BF16)
+                out_ref[rows, :] = tile
                 if step:
-                    r.conv_out[rows, :] = tile
-                    src, dst = r.conv_out.at[rows], r.conv_in.at[z]
+                    src, dst = out_ref.at[rows], r.conv_in.at[z]
                     send(("za", k), chan_copy(k, src, dst, step, block))
                 else:
                     r.conv_in[z] = tile
@@ -698,10 +698,32 @@
                 dst = r.conv_in.at[source]
                 chan_copy(k, dst, dst, step, source).wait_recv()
 
-        to_tokens(1)
-        gather_forward(1)
+        to_tokens(1, r.conv_out)
+        load_cot.wait()
+        gather_start(0, r.cotv)
         load_wout.wait()
+        def gate_cols(at):
+            cols = pl.ds(at, 128)
+            r.gate_out[:, cols] = mix(cols)[1]
+
+        tiles(128, width, gate_cols)
+
+        def grad_hidden(at, carry):
+            slot = lax.rem(at, 2)
+            down_weights(at, slot).wait()
+            r.pre_send[at] = mm_nt(r.cotv[...], r.win[1, span(slot, ffc), :], out=BF16)
+            down_weights(lax.rem(at + 2, groups), slot).start()
+            return carry
+
+        lax.fori_loop(0, groups, grad_hidden, 0)
         wait_tokens(1)
+
+        def seq_gather(step, source, to):
+            rows = r.n1_all.at[span(source, tokens)]
+            return remote(rows, rows, r.zg_s.at[step - 1], r.zg_r.at[step - 1], seq=to)
+
+        for step in range(1, blocks):
+            send("n1", seq_gather(step, z, block_at(step)))
 
         def conv_cols(at):
             return r.conv_in[
@@ -739,32 +761,27 @@
             r.half[rows, :] = (xhat * r.gain2[...]).astype(BF16)
 
         tiles(32, tokens, norm2)
-        drain(("ag", 1))
-        gather_local(1, r.turn).wait()
         turned(r.half, r.turn)
-        gather_start(2, r.turn)
         r.gn2[...] = jnp.zeros((tokens, width), F32)
 
         def plane_copy(k, src, dst, at, to):
             return remote(src, dst, r.pa_s.at[k, at], r.pa_r.at[k, at], batch=to)
 
-        def chunk_copies(at, to):
-            return (
-                plane_copy(0, r.hid_send.at[at], r.hid_own.at[:, span(b, tokens)], at, to),
-                plane_copy(1, r.pre_send.at[at], r.pre_own.at[span(b, tokens)], at, to),
-            )
+        def hidden_copy(at, to):
+            return plane_copy(0, r.hid_send.at[at], r.hid_own.at[:, span(b, tokens)], at, to)
+
+        def pre_copy(at, to):
+            return plane_copy(1, r.pre_send.at[at], r.pre_own.at[span(b, tokens)], at, to)
 
         def chunk(at, carry):
             slot = lax.rem(at, 2)
             where = span(slot, ffc)
-            for copy in ffn_weights(at, slot):
-                copy.wait()
-            r.gmix[0:tokens, 0:ffc] = mm(r.half[...], r.win[0, :, where])
-            r.gmix[0:tokens, ffc : 2 * ffc] = mm_nt(r.cotv[...], r.win[1, where, :])
+            up_weights(at, slot).wait()
+            r.gres[:, 0:ffc] = mm(r.half[...], r.win[0, :, where])
 
             def act(row):
-                rows = pl.ds(row, 64)
-                pre = r.gmix[rows, 0:ffc]
+                rows = pl.ds(row, 32)
+                pre = r.gres[rows, 0:ffc]
                 square = pre * pre
                 bent = jnp.tanh(pre * (GELU_SCALE + GELU_SCALE * GELU_CUBIC * square))
                 upper = 0.5 + 0.5 * bent
@@ -772,29 +789,29 @@
                     GELU_SCALE + 3.0 * GELU_SCALE * GELU_CUBIC * square
                 )
                 r.hid_buf[rows, :] = (pre * upper).astype(BF16)
-                r.pre_send[at, rows, :] = (r.gmix[rows, ffc : 2 * ffc] * slope).astype(BF16)
-
-            tiles(64, tokens, act)
+                r.pre_send[at, rows, :] = (r.pre_send[at, rows, :].astype(F32) * slope).astype(BF16)
+
+            tiles(32, tokens, act)
             r.hid_send[at] = r.hid_buf[...].T
 
             @pl.when(at < groups - 1)
             def _():
-                for copy in chunk_copies(at, lax.rem(b + 1 + at, groups)):
-                    copy.start()
-
+                hidden_copy(at, lax.rem(b + 1 + at, groups)).start()
+
+            down_weights(at, slot).wait()
             r.res[...] += mm(r.hid_buf[...], r.win[1, where, :])
             r.gn2[...] += mm_nt(r.pre_send[at], r.win[0, :, where])
 
             @pl.when(at < groups - 2)
             def _():
-                for copy in ffn_weights(at + 2, slot):
-                    copy.start()
+                up_weights(at + 2, slot).start()
+                down_weights(at + 2, slot).start()
 
             return carry
 
         lax.fori_loop(0, groups, chunk, 0)
         for at in range(peers):
-            sent.setdefault("ffn", []).extend(chunk_copies(at, group_at(1 + at)))
+            sent.setdefault("ffn", []).append(hidden_copy(at, group_at(1 + at)))
 
         def pool_cot():
             return [load(r.win_sem.at[half], r.cot_land.at[half], r.win.at[half]) for half in range(2)]
@@ -809,9 +826,7 @@
                 for at in range(groups)
             ]
 
-        gather_local(0, r.cotv).wait()
-        gather_finish(0)
-        pool = pool_cot()
+        gather_forward(0)
         r.hid_own[:, span(b, tokens)] = r.hid_send[groups - 1]
         r.pre_own[span(b, tokens), :] = r.pre_send[groups - 1]
 
@@ -835,26 +850,29 @@
             grad = mm_nt(r.gbr_pair[mine, :], r.wout[span(block, own), :])
             glong = (grad * r.gate_out[:, cols]).astype(BF16)
             r.glong[:, cols] = glong
-            r.gmix[0:tokens, cols] = grad * r.long[:, cols]
+            r.ggb[:, cols] = grad.astype(BF16)
+            r.long[:, cols] = grad * r.long[:, cols]
             r.sum_bias[:, cols] = jnp.sum(
                 glong.astype(F32) * r.sig[:, cols].astype(F32), axis=0, keepdims=True
             )
 
-        to_channels(2, r.glong, gated_back)
+        to_channels(2, r.ggb, gated_back)
+
+        gather_start(1, r.turn)
 
         branch_copy.wait_recv()
         gated_copy.wait_recv()
-        for step in list(range(1, chips)) + [0]:
-            to = lax.rem(chip + step, chips)
-            part = mm(r.gated_pair[span(to, share), :], r.gbr_pair[...])
+
+        def out_copy(step, to):
+            sems = r.wo_s.at[0, step - 1], r.wo_r.at[0, step - 1]
+            return remote(r.out_send.at[step - 1], r.out_land.at[step - 1], *sems, batch=to * 2 + core)
+
+        for step in range(chips):
+            part = mm(r.gated_pair[span(lax.rem(chip + step, chips), share), :], r.gbr_pair[...])
             if step:
-                at = step - 1
-                r.out_send[at] = part.astype(BF16)
-                sems = r.wo_s.at[0, at], r.wo_r.at[0, at]
-                send("out", remote(r.out_send.at[at], r.out_land.at[at], *sems, batch=to * 2 + core))
+                r.out_send[step - 1] = part.astype(BF16)
             else:
-                r.out_own[...] = part
-        gather_forward(2)
+                r.xhat2[share : 2 * share, :] = part
 
         near = z + 1 - 2 * lax.rem(z, 2)
         far = block_at(2)
@@ -884,9 +902,8 @@
             reduce_second(k, refs).wait_recv()
             refs[4][...] += refs[3][...].astype(F32)
 
-        down_refs = (r.down_send, r.down_land, r.down_next, r.down_last, r.down_own)
-        up_refs = (r.up_send, r.up_land, r.up_next, r.up_last, r.up_own)
-        in_refs = (r.in_send, r.in_land, r.in_next, r.in_last, r.in_own)
+        down_refs = (r.down_send, r.down_land, r.down_next, r.down_last, r.xhat2.at[0:down_rows])
+        up_refs = (r.up_send, r.up_land, r.up_next, r.up_last, r.gate_out.at[:, 0:ffc])
 
         def wait_plane(k, dst_of):
             for at in range(peers):
@@ -908,12 +925,47 @@
             return part
 
 
+        gather_local(0, r.cotv).wait()
+        gather_finish(0)
+        pool = pool_cot()
+
+        for step in range(1, blocks):
+            source = block_at(blocks - step)
+            seq_gather(step, source, source).wait_recv()
+        for copy in own_loads:
+            copy.wait()
+
+        def proj_rows(at):
+            r.ext_c[pl.ds(pl.multiple_of(at + spare, spare), tokens), :] = mm(
+                r.n1_all[pl.ds(at, tokens), :], r.win[2, :, 0 : 3 * own], out=BF16
+            )
+
+        tiles(tokens, length, proj_rows)
+
+        def own_cols(part, at):
+            return pl.ds(pl.multiple_of(part * width + z * own + at, 128), 128)
+
+        def mix_own(part, at, first, rows):
+            wide = r.ext_c[pl.ds(first, rows + spare), part * own + at : part * own + at + 128].astype(F32)
+            short = r.short[:, own_cols(part, at)].astype(F32)
+            lags = [wide[spare - lag : spare - lag + rows] for lag in range(3)]
+            return short[0:1] * lags[0] + short[1:2] * lags[1] + short[2:3] * lags[2]
+
         wait_channels(2)
+
+        def long_rows(first):
+            rows = pl.ds(first, tokens)
+            for at in range(0, own, 128):
+                cols = slice(at, at + 128)
+                gate = mix_own(0, at, first, tokens)
+                r.glong_c[rows, cols] = (r.chan[rows, cols].astype(F32) * gate).astype(BF16)
+
+        tiles(tokens, length, long_rows)
 
         def grad_spec(at):
             rows = pl.ds(at, tokens)
-            real = mm(r.cs[rows, :], r.chan[...])
-            imag = -mm(r.sn[rows, :], r.chan[...])
+            real = mm(r.cs[rows, :], r.glong_c[0:length, :])
+            imag = -mm(r.sn[rows, :], r.glong_c[0:length, :])
             hre, him = r.hre[rows, :], r.him[rows, :]
             r.yre[rows, :] = (hre * real + him * imag).astype(BF16)
             r.yim[rows, :] = (him * real - hre * imag).astype(BF16)
@@ -925,8 +977,59 @@
             r.qim[rows, :] = ((both_re * turn_im - both_im * turn_re) * scale).astype(BF16)
 
         tiles(tokens, length, grad_spec)
-        drain(("za", 1))
-        to_tokens(3)
+        to_tokens(3, r.gconv_c)
+        for at in range(peers):
+            send("ffn", pre_copy(at, group_at(1 + at)))
+
+        def proj_back(first):
+            rows = pl.ds(first, tokens + spare)
+            for at in range(0, own, 128):
+                cols = slice(at, at + 128)
+                gate_in = mix_own(1, at, first, tokens + spare)
+                values = mix_own(2, at, first, tokens + spare)
+                bias = r.bias[:, own_cols(0, at)]
+                signal = (values * gate_in).astype(BF16).astype(F32)
+                long = r.conv_out[rows, cols].astype(F32) + bias * signal
+                grad_signal = r.gconv_c[rows, cols].astype(F32) + bias * r.glong_c[rows, cols].astype(F32)
+                parts = (r.chan[rows, cols].astype(F32) * long, grad_signal * values, grad_signal * gate_in)
+                for part, grad in enumerate(parts):
+                    short = r.short[:, own_cols(part, at)].astype(F32)
+                    total = (
+                        short[0:1] * grad[0:tokens]
+                        + short[1:2] * grad[1 : tokens + 1]
+                        + short[2:3] * grad[2 : tokens + 2]
+                    )
+                    r.gproj_c[pl.ds(first, tokens), part * own + at : part * own + at + 128] = total.astype(BF16)
+
+        tiles(tokens, length, proj_back)
+
+        def in_part(group):
+            return mm_tn(r.n1_all[:, span(group, share)], r.gproj_c[...])
+
+        for at in range(chips):
+            r.in_send[at] = in_part(at * 2 + 1 - core).astype(BF16)
+        in_pair = pair_copy(2, r.in_send, r.in_pair)
+        send("in_pair", in_pair)
+        for copy in pool:
+            copy.wait()
+        wait_plane(0, lambda at: r.hid_own.at[:, span(at, tokens)])
+        reduce_send(0, down_refs, down_part)
+        in_pair.wait_recv()
+        drain("in_pair")
+
+        def in_copy(step, to):
+            sems = r.wi_s.at[step - 1], r.wi_r.at[step - 1]
+            return remote(r.in_send.at[step - 1], r.in_land.at[step - 1], *sems, batch=to * 2 + core)
+
+        for step in list(range(1, chips)) + [0]:
+            to = lax.rem(chip + step, chips)
+            part = in_part(to * 2 + core) + r.in_pair[to].astype(F32)
+            if step:
+                r.in_send[step - 1] = part.astype(BF16)
+                send("in", in_copy(step, to))
+            else:
+                r.in_own[...] = part
+
         r.w12[...] = jnp.zeros((net_rows, 128), F32)
         r.sum_w3[...] = jnp.zeros((filt, own), F32)
         for at in range(0, length, tokens):
@@ -972,25 +1075,23 @@
             sems = r.wo_s.at[1, step - 1], r.wo_r.at[1, step - 1]
             return remote(r.outz_send.at[span(to, rows_out)], r.outz_land.at[step - 1], *sems, seq=to)
 
-        for step in range(1, chips):
-            land = r.out_land.at[step - 1]
-            sems = r.wo_s.at[0, step - 1], r.wo_r.at[0, step - 1]
-            source = lax.rem(chip + chips - step, chips) * 2 + core
-            remote(land, land, *sems, batch=source).wait_recv()
-        total = r.out_own[...]
-        for step in range(chips - 1):
-            total = total + r.out_land[step].astype(F32)
-        r.out_own[...] = total
-        r.outz_send[...] = total.astype(BF16)
-        for step in range(1, blocks):
-            send("outz", outz_copy(step, block_at(step)))
-        r.outz_own[...] = r.out_own[span(z, rows_out), :]
-
-        wait_tokens(3)
 
         def short_sums(cols, grad, lags):
             for lag in range(3):
                 r.sum_short[lag : lag + 1, cols] = jnp.sum(grad * lags[lag], axis=0, keepdims=True)
+
+        def back_cols(cols, grad, lags):
+            short_sums(cols, grad, lags)
+            r.ghalo[:, cols] = grad[0:8]
+            short = r.short[:, cols].astype(F32)
+            longer = jnp.concatenate([grad, jnp.zeros((8, 128), F32)], axis=0)
+            total = (
+                short[0:1] * grad
+                + short[1:2] * longer[1 : tokens + 1]
+                + short[2:3] * longer[2 : tokens + 2]
+            )
+            r.gproj[:, cols] = total.astype(BF16)
+            r.tail[:, cols] = total[tokens - 16 :]
 
         def mixed_cols(at):
             cols = pl.ds(at, 128)
@@ -999,25 +1100,51 @@
             value_cols = pl.ds(pl.multiple_of(2 * width + at, 128), 128)
             gate_lags, gate_in = mix(gate_cols)
             value_lags, values = mix(value_cols)
-            grad_gate = grad_signal * values
-            r.gmix[0:tokens, gate_cols] = grad_gate
-            short_sums(gate_cols, grad_gate, gate_lags)
-            grad_value = grad_signal * gate_in
-            r.gmix[0:tokens, value_cols] = grad_value
-            short_sums(value_cols, grad_value, value_lags)
-
+            back_cols(gate_cols, grad_signal * values, gate_lags)
+            back_cols(value_cols, grad_signal * gate_in, value_lags)
+
+        def gate_back(at):
+            cols = pl.ds(at, 128)
+            back_cols(cols, r.long[:, cols], lags_at(cols))
+
+        drain(("forward", 0))
+        tiles(128, width, gate_back)
+        wait_tokens(3)
         tiles(128, width, mixed_cols)
-        halo = remote(
-            r.gmix.at[0:8], r.gmix.at[tokens : tokens + 8],
-            r.halo_s.at[1], r.halo_r.at[1], seq=block_at(blocks - 1),
-        )
+        halo = remote(r.ghalo, r.ghalo_in, r.halo_s.at[1], r.halo_r.at[1], seq=block_at(blocks - 1))
         send("halo", halo)
-
-        def gate_short(at):
-            cols = pl.ds(at, 128)
-            short_sums(cols, r.gmix[0:tokens, cols], lags_at(cols))
-
-        tiles(128, width, gate_short)
+        gather_forward(1)
+        halo.wait_recv()
+        later = r.ghalo_in[...] * jnp.where(z < blocks - 1, 1.0, 0.0)
+
+        def tail_cols(at):
+            cols = slice(at, at + width)
+            short = r.short[:, cols].astype(F32)
+            row = lax.broadcasted_iota(jnp.int32, (16, width), 0)
+            last = short[1:2] * later[0:1, cols] + short[2:3] * later[1:2, cols]
+            total = r.tail[:, cols] + jnp.where(row == 15, last, 0.0)
+            total = total + jnp.where(row == 14, short[2:3] * later[0:1, cols], 0.0)
+            r.gproj[tokens - 16 :, cols] = total.astype(BF16)
+
+        for part in range(3):
+            tail_cols(part * width)
+
+        def spread(k, own_ref, out_ref, size):
+            for at in range(peers):
+                to = group_at(1 + at)
+                src, dst = own_ref.at[span(to, rows_out)], out_ref.at[:, span(b, size)]
+                send("spread", remote(src, dst, r.tr_s.at[k, at], r.tr_r.at[k, at], batch=to))
+            return load(r.local_sem.at[14 + k], own_ref.at[span(b, rows_out)], out_ref.at[:, span(b, size)])
+
+        def spread_finish(k, copy, out_ref, size):
+            for at in range(peers):
+                source = group_at(groups - 1 - at)
+                dst = out_ref.at[:, span(source, size)]
+                remote(dst, dst, r.tr_s.at[k, at], r.tr_r.at[k, at], batch=source).wait_recv()
+            copy.wait()
+
+        for step in range(1, chips):
+            send("out", out_copy(step, lax.rem(chip + step, chips)))
         small_z_wait(0, lambda step: r.w12_z.at[step - 1])
         net = r.w12[...]
         for step in range(zpeers):
@@ -1031,47 +1158,10 @@
         r.w3_part[...] = part
         r.w3_all[z, span(b, w3_rows), :] = part
         small_send(2, lambda to: r.w3_part, lambda at: r.w3_all.at[z, span(b, w3_rows)])
-        halo.wait_recv()
-        r.gmix[tokens:, :] = r.gmix[tokens:, :] * jnp.where(z < blocks - 1, 1.0, 0.0)
-
-        drain(("forward", 0))
-        for step in list(range(1, groups)) + [0]:
-            group = group_at(step)
-
-            def proj_cols(at, group=group):
-                cols = pl.ds(pl.multiple_of(group * inc + at, 128), 128)
-                short = r.short[:, cols].astype(F32)
-                grads = [r.gmix[lag : lag + tokens, cols] for lag in range(3)]
-                total = short[0:1] * grads[0] + short[1:2] * grads[1] + short[2:3] * grads[2]
-                r.gproj[:, cols] = total.astype(BF16)
-
-            tiles(128, inc, proj_cols)
-            mine = r.gproj_own.at[span(b, tokens)]
-            if step:
-                send("gproj", plane_copy(2, r.gproj.at[:, span(group, inc)], mine, step - 1, group))
-            else:
-                r.gproj_own[span(b, tokens), :] = r.gproj[:, span(group, inc)]
-
-        def spread(k, own_ref, out_ref, size):
-            for at in range(peers):
-                to = group_at(1 + at)
-                src, dst = own_ref.at[span(to, rows_out)], out_ref.at[:, span(b, size)]
-                send("spread", remote(src, dst, r.tr_s.at[k, at], r.tr_r.at[k, at], batch=to))
-            return load(r.local_sem.at[14 + k], own_ref.at[span(b, rows_out)], out_ref.at[:, span(b, size)])
-
-        def spread_finish(k, copy, out_ref, size):
-            for at in range(peers):
-                source = group_at(groups - 1 - at)
-                dst = out_ref.at[:, span(source, size)]
-                remote(dst, dst, r.tr_s.at[k, at], r.tr_r.at[k, at], batch=source).wait_recv()
-            copy.wait()
-
-        for copy in pool:
-            copy.wait()
-        wait_plane(0, lambda at: r.hid_own.at[:, span(at, tokens)])
-        reduce_send(0, down_refs, down_part)
-        gather_local(2, r.turn).wait()
-        gather_finish(2)
+        reduce_next(0, down_refs)
+        gather_local(1, r.turn).wait()
+        gather_finish(1)
+        drain(("forward", 1))
         pool = pool_turned(r.n2_land)
         small_wait(1, lambda at: r.w12_plane.at[at])
         net = r.w12_sum[...]
@@ -1086,27 +1176,33 @@
         for copy in pool:
             copy.wait()
         wait_plane(1, lambda at: r.pre_own.at[span(at, tokens)])
-        reduce_next(0, down_refs)
         reduce_send(1, up_refs, turned_part(r.pre_own))
-        win_loads = [(block, load_win(block)) for block in range(2)]
-        for step in range(1, blocks):
-            outz_copy(step, block_at(blocks - step)).wait_recv()
-        total = r.outz_own[...]
-        for step in range(zpeers):
-            total = total + r.outz_land[step].astype(F32)
-        r.outz_own[...] = total
-        store_out = load(r.local_sem.at[11], r.outz_own, r.grad_w_out)
-        reduce_finish(0, down_refs)
-        store_down = load(r.local_sem.at[9], r.down_own, r.grad_w_down)
+        win_loads = [(block, load_win(block)) for block in range(3)]
+        for step in range(1, chips):
+            in_copy(step, lax.rem(chip + step, chips)).wait_recv()
+        total = r.in_own[...]
+        for step in range(chips - 1):
+            total = total + r.in_land[step].astype(F32)
+        r.in_own[...] = total
+
+        def in_spread(step, part, block, to):
+            src = r.in_own.at[span(to, rows_out), part * own : (part + 1) * own]
+            dst = r.grad_w_in.at[:, pl.ds(pl.multiple_of(part * width + block * own, own), own)]
+            if step == 0:
+                return pltpu.make_async_copy(src, dst, r.load_sem.at[10 + part])
+            return remote(src, dst, r.ti_s.at[step - 1, part], r.ti_r.at[step - 1, part], seq=to)
+
+        for part in range(3):
+            for step in range(1, blocks):
+                send("in_spread", in_spread(step, part, z, block_at(step)))
+            in_spread(0, part, z, z).start()
         for _, copy in win_loads:
             copy.wait()
         r.gn2[...] = mm_nt(r.gproj[:, :width], r.win[0])
         r.gn2[...] += mm_nt(r.gproj[:, width : 2 * width], r.win[1])
+        r.gn2[...] += mm_nt(r.gproj[:, 2 * width :], r.win[2])
+
         reduce_next(1, up_refs)
-        gather_finish(1)
-        pool = pool_turned(r.n1_land)
-        r.gn2[...] += mm_nt(r.gproj[:, 2 * width :], r.win[2])
-
         def norm1_back(at, total):
             rows = pl.ds(pl.multiple_of(at * 32, 32), 32)
             grad, inverse = r.gn2[rows, :], r.inv1[rows, 0:1]
@@ -1130,12 +1226,19 @@
         small_send(3, lambda to: r.small_send.at[to], lambda at: r.small_land.at[b])
         r.small_land[b] = r.small_send[b]
         store_tokens = load(r.local_sem.at[13], r.res, r.tokens_grad)
-        for copy in pool:
-            copy.wait()
-        wait_plane(2, lambda at: r.gproj_own.at[span(at, tokens)])
-        reduce_send(2, in_refs, turned_part(r.gproj_own))
-        reduce_finish(1, up_refs)
-        spread_up = spread(0, r.up_own, r.grad_w_up, ffc)
+        reduce_finish(0, down_refs)
+        store_down = load(r.local_sem.at[9], down_refs[4], r.grad_w_down)
+        for step in range(1, chips):
+            out_copy(step, lax.rem(chip + step, chips)).wait_recv()
+        total = r.xhat2[share : 2 * share, :]
+        for step in range(chips - 1):
+            total = total + r.out_land[step].astype(F32)
+        r.xhat2[share : 2 * share, :] = total
+        r.outz_send[...] = total.astype(BF16)
+        for step in range(1, blocks):
+            send("outz", outz_copy(step, block_at(step)))
+        r.outz_own[...] = r.xhat2[pl.ds(pl.multiple_of(share + z * rows_out, rows_out), rows_out), :]
+
         for at in range(peers):
             source = group_at(groups - 1 - at)
             dst = r.small_land.at[source]
@@ -1145,10 +1248,15 @@
             small = small + r.small_land[group]
         r.small_sum[...] = small
         small_z_send(2, r.small_sum, lambda step: r.small_z.at[step - 1])
-        reduce_next(2, in_refs)
-        reduce_finish(2, in_refs)
-        spread_in = spread(1, r.in_own, r.grad_w_in, inc)
-
+        reduce_finish(1, up_refs)
+        spread_up = spread(0, up_refs[4], r.grad_w_up, ffc)
+        for step in range(1, blocks):
+            outz_copy(step, block_at(blocks - step)).wait_recv()
+        total = r.outz_own[...]
+        for step in range(zpeers):
+            total = total + r.outz_land[step].astype(F32)
+        r.outz_own[...] = total
+        store_out = load(r.local_sem.at[11], r.outz_own, r.grad_w_out)
         def chosen(value, size):
             picked = value[:, :size]
             for block in range(1, blocks):
@@ -1179,7 +1287,11 @@
                 r.short_all[lag : lag + 1, third * share : (third + 1) * share] = small[row : row + 1]
         r.grad_short[...] = chosen(r.short_all[0:3, :], 3 * rows_out)
         spread_finish(0, spread_up, r.grad_w_up, ffc)
-        spread_finish(1, spread_in, r.grad_w_in, inc)
+        for part in range(3):
+            for step in range(1, blocks):
+                source = block_at(blocks - step)
+                in_spread(step, part, source, source).wait_recv()
+            in_spread(0, part, z, z).wait()
         store_layer.wait()
         store_down.wait()
         store_out.wait()
@@ -1205,19 +1317,44 @@
 
 def settled(values):
     count = len(values)
+    large = [at for at, value in enumerate(values) if value.size >= 1 << 15]
 
     def copy_all(*refs):
-        for source, target in zip(refs[:count], refs[count:]):
-            target[...] = source[...].reshape(target.shape)
-
+        sources, targets, held = refs[:count], refs[count : 2 * count], refs[2 * count : -1]
+        sems = refs[-1]
+        copies = [
+            pltpu.make_async_copy(sources[at], held[k], sems.at[0, k]) for k, at in enumerate(large)
+        ]
+        for copy in copies:
+            copy.start()
+        for at in range(count):
+            if at not in large:
+                if at == count - 1:
+                    targets[at][...] = sources[at][...].T
+                else:
+                    targets[at][...] = sources[at][...].reshape(targets[at].shape)
+        stores = []
+        for k, at in enumerate(large):
+            copies[k].wait()
+            stores.append(pltpu.make_async_copy(held[k], targets[at], sems.at[1, k]))
+            stores[-1].start()
+        for copy in stores:
+            copy.wait()
+
+    specs = [
+        pl.BlockSpec(memory_space=pl.ANY if at in large else pltpu.VMEM) for at in range(count)
+    ]
     return pl.pallas_call(
         copy_all,
         out_shape=[
             jax.ShapeDtypeStruct(value.shape[1:] if value.shape[0] == 1 else value.shape, value.dtype)
-            for value in values
-        ],
-        in_specs=[pl.BlockSpec(memory_space=pltpu.VMEM)] * count,
-        out_specs=[pl.BlockSpec(memory_space=pltpu.VMEM)] * count,
+            for value in values[:-1]
+        ]
+        + [jax.ShapeDtypeStruct(values[-1].shape[::-1], values[-1].dtype)        ],
+        in_specs=specs,
+        out_specs=specs,
+        scratch_shapes=[pltpu.VMEM(values[at].shape, values[at].dtype) for at in large]
+        + [pltpu.SemaphoreType.DMA((2, len(large)))],
     )(*values)
 
 
@@ -1297,7 +1434,7 @@
         )
     )
     layer_out, tokens_grad, w_in, w_out, w_up, w_down, gain1, gain2, bias, short, w1, w2, w3 = out
-    return layer_out[None], tokens_grad[None], (gain1, short, w1, w2, w3, bias, gain2), (w_in, w_out, w_up, w_down)
+    return layer_out[None], tokens_grad[None], (gain1, short, w1, w2, w3.T, bias, gain2), (w_in, w_out, w_up, w_down)
 
 
 def on_device(*args):

time: 225 us -> 204 us (0.907)
  Pallas kernels: 222 us -> 203 us
    pallas_call x1, Pallas kernels: 219 us -> 199 us  [call(): pl.pallas_call(kernel, out_shape=[jax.ShapeDtypeStruct(shape, dtype) for...]
where the time goes in v2:
time: 204 us
  Pallas kernels  203 us (100%)
    pallas_call x1, Pallas kernels, call(): pl.pallas_call(kernel, out_shape=[jax.ShapeDtypeStruct(shape, dtype) for...  199 us
    pallas_call x1, Pallas kernels, settled(): pl.pallas_call(copy_all, out_shape=[jax.ShapeDtypeStruct(value.shape[1:]...  4.44 us

profile of v2, /device:TPU:1, one launch (start us, length us, event | category | flops | bytes accessed | tf_op | source)
XLA Modules:
  0.0 203.9 jit_solution(16472334324877529722)
XLA Ops:
  0.7 198.6 %shard_map.273 = (bf16[256,1024]{1,0:T(8,128)(2,1)}, f32[256,1024]{1,0:T(8,128)}, f32[32,3072]{1,0:T(8,128)}, f32[32,1024]{1,0:T(8,128)}, f32[32,4096]{1,0:T(8,1...) custom-call(bf16[256,1024]{1,0:T(8,128)(2,1)} %bitcast.9, ...), custom_call_target="tpu_custom_call" | custom-call | tf_op jit(solution)/shard_map/pallas_call | solution.py:1303
  199.3 4.4 %shard_map.274 = (bf16[256,1024]{1,0:T(8,128)(2,1)}, f32[256,1024]{1,0:T(8,128)}, f32[32,3072]{1,0:T(8,128)}, f32[32,1024]{1,0:T(8,128)}, f32[32,4096]{1,0:T(8,1...) custom-call(bf16[256,1024]{1,0:T(8,128)(2,1)} %get-tuple-element.39., ...), custom_call_target="tpu_custom_call" | custom-call | tf_op jit(solution)/shard_map/pallas_call | solution.py:1347

commit v3 on v2

--- a/solution.py
+++ b/solution.py
@@ -432,6 +432,32 @@
         sibling = chip * 2 + (1 - core)
         sent = {}
 
+        chip_x, chip_y = lax.rem(chip, 2), lax.div(chip, 2)
+
+        def flipped(turn_x, turn_y):
+            x = chip_x + turn_x - 2 * chip_x * turn_x
+            y = chip_y + turn_y - 2 * chip_y * turn_y
+            return y * 2 + x
+
+        def partner(way):
+            return flipped(1 - way % 2, (way + 1) // 2)
+
+        def way_of(step):
+            return 2 if step == 2 else step + core - 2 * step * core
+
+        def partner_at(way):
+            return flipped(1 - lax.rem(way, 2), lax.div(way + 1, 2))
+
+        def peer(at):
+            at = jnp.int32(at)
+            late, last = lax.div(at, 4), lax.div(at, 6)
+            way = (1 - late) * lax.rem(at + core, 2) + late * 2
+            to_core = (1 - late) * lax.div(at, 2) + late * (at - 4)
+            to_chip = flipped((1 - last) * (1 - lax.rem(way, 2)), (1 - last) * lax.div(way + 1, 2))
+            own_chip = (7 - at) * (1 - core) + (at - 6) * core
+            group = to_chip * 2 + (1 - last) * to_core + last * own_chip
+            return group, (1 - last) * (way * 2 + to_core) + last * 6, (1 - last) * (way * 2 + core) + last * 6
+
         def group_at(step):
             return lax.rem(b + step, groups)
 
@@ -464,7 +490,7 @@
 
         def load(sem, src, dst):
             copy = pltpu.make_async_copy(src, dst, sem)
-            copy.start()
+            copy.start(priority=1)
             return copy
 
         def load_win(block):
@@ -497,11 +523,12 @@
             return pltpu.make_async_copy(src, slots[k](b), r.local_sem.at[k])
 
         def gather_start(k, src):
-            for step in range(1, chips):
-                to = lax.rem(chip + step, chips) * 2 + core
-                send(("ag", k), gather_copy(k, step - 1, src, slots[k](b), to))
+            for step in range(chips - 1):
+                way = way_of(step)
+                to = partner_at(jnp.int32(way)) * 2 + core
+                send(("ag", k), gather_copy(k, way, src, slots[k](b), to))
             send(("ag", k), gather_copy(k, chips - 1, src, slots[k](b), sibling))
-            gather_local(k, src).start()
+            gather_local(k, src).start(priority=1)
 
         def stage(k, step):
             if k == 0:
@@ -511,7 +538,7 @@
         def gather_forward(k):
             staged = []
             for step in range(1, chips):
-                slot = slots[k](lax.rem(chip + chips - step, chips) * 2 + core)
+                slot = slots[k](partner(step - 1) * 2 + core)
                 gather_copy(k, step - 1, slot, slot, sibling).wait_recv()
                 staged.append((slot, load(r.stage_sem.at[step - 1], slot, stage(k, step))))
             for step, (slot, copy) in enumerate(staged, 1):
@@ -521,7 +548,7 @@
 
         def gather_finish(k):
             for step in range(chips):
-                slot = slots[k](lax.rem(chip + chips - step, chips) * 2 + 1 - core)
+                slot = slots[k]((partner(step - 1) if step else chip) * 2 + 1 - core)
                 gather_copy(k, chips - 1 + step, slot, slot, sibling).wait_recv()
 
         def turned(value_ref, out_ref):
@@ -577,20 +604,20 @@
         r.ext_c[length + spare :, :] = jnp.zeros((spare, 3 * own), BF16)
 
         def up_weights(at, slot):
-            group = lax.rem(b + 1 + at, groups)
+            group = peer(at)[0]
             return pltpu.make_async_copy(
                 r.w_up.at[:, span(group, ffc)], r.win.at[0, :, span(slot, ffc)], r.ffn_sem.at[slot, 0]
             )
 
         def down_weights(at, slot):
-            group = lax.rem(b + 1 + at, groups)
+            group = peer(at)[0]
             return pltpu.make_async_copy(
                 r.w_down.at[span(group, ffc)], r.win.at[1, span(slot, ffc)], r.ffn_sem.at[slot, 1]
             )
 
         for at in range(2):
-            down_weights(at, at).start()
-            up_weights(at, at).start()
+            down_weights(at, at).start(priority=1)
+            up_weights(at, at).start(priority=1)
 
         halo.wait_recv()
         r.ext[0:16, :] = (r.halo_in[...].astype(F32) * jnp.where(z > 0, 1.0, 0.0)).astype(BF16)
@@ -634,6 +661,8 @@
             tiles(128, own, body)
 
         to_channels(0, r.sig, signal_block)
+        load_cot.wait()
+        gather_start(0, r.cotv)
 
         load_w3.wait()
         load_fade.wait()
@@ -699,8 +728,14 @@
                 chan_copy(k, dst, dst, step, source).wait_recv()
 
         to_tokens(1, r.conv_out)
-        load_cot.wait()
-        gather_start(0, r.cotv)
+
+        def seq_gather(step, source, to):
+            rows = r.n1_all.at[span(source, tokens)]
+            return remote(rows, rows, r.zg_s.at[step - 1], r.zg_r.at[step - 1], seq=to)
+
+        for step in range(1, blocks):
+            send("n1", seq_gather(step, z, block_at(step)))
+
         load_wout.wait()
         def gate_cols(at):
             cols = pl.ds(at, 128)
@@ -712,18 +747,11 @@
             slot = lax.rem(at, 2)
             down_weights(at, slot).wait()
             r.pre_send[at] = mm_nt(r.cotv[...], r.win[1, span(slot, ffc), :], out=BF16)
-            down_weights(lax.rem(at + 2, groups), slot).start()
+            down_weights(lax.rem(at + 2, groups), slot).start(priority=1)
             return carry
 
         lax.fori_loop(0, groups, grad_hidden, 0)
         wait_tokens(1)
-
-        def seq_gather(step, source, to):
-            rows = r.n1_all.at[span(source, tokens)]
-            return remote(rows, rows, r.zg_s.at[step - 1], r.zg_r.at[step - 1], seq=to)
-
-        for step in range(1, blocks):
-            send("n1", seq_gather(step, z, block_at(step)))
 
         def conv_cols(at):
             return r.conv_in[
@@ -764,14 +792,15 @@
         turned(r.half, r.turn)
         r.gn2[...] = jnp.zeros((tokens, width), F32)
 
-        def plane_copy(k, src, dst, at, to):
-            return remote(src, dst, r.pa_s.at[k, at], r.pa_r.at[k, at], batch=to)
-
-        def hidden_copy(at, to):
-            return plane_copy(0, r.hid_send.at[at], r.hid_own.at[:, span(b, tokens)], at, to)
-
-        def pre_copy(at, to):
-            return plane_copy(1, r.pre_send.at[at], r.pre_own.at[span(b, tokens)], at, to)
+        def plane_copy(k, src, dst, at):
+            to, send_at, recv_at = peer(at)
+            return remote(src, dst, r.pa_s.at[k, send_at], r.pa_r.at[k, recv_at], batch=to)
+
+        def hidden_copy(at):
+            return plane_copy(0, r.hid_send.at[at], r.hid_own.at[:, span(b, tokens)], at)
+
+        def pre_copy(at):
+            return plane_copy(1, r.pre_send.at[at], r.pre_own.at[span(b, tokens)], at)
 
         def chunk(at, carry):
             slot = lax.rem(at, 2)
@@ -796,7 +825,7 @@
 
             @pl.when(at < groups - 1)
             def _():
-                hidden_copy(at, lax.rem(b + 1 + at, groups)).start()
+                hidden_copy(at).start()
 
             down_weights(at, slot).wait()
             r.res[...] += mm(r.hid_buf[...], r.win[1, where, :])
@@ -804,14 +833,14 @@
 
             @pl.when(at < groups - 2)
             def _():
-                up_weights(at + 2, slot).start()
-                down_weights(at + 2, slot).start()
+                up_weights(at + 2, slot).start(priority=1)
+                down_weights(at + 2, slot).start(priority=1)
 
             return carry
 
         lax.fori_loop(0, groups, chunk, 0)
         for at in range(peers):
-            sent.setdefault("ffn", []).append(hidden_copy(at, group_at(1 + at)))
+            sent.setdefault("ffn", []).append(hidden_copy(at))
 
         def pool_cot():
             return [load(r.win_sem.at[half], r.cot_land.at[half], r.win.at[half]) for half in range(2)]
@@ -863,12 +892,14 @@
         branch_copy.wait_recv()
         gated_copy.wait_recv()
 
-        def out_copy(step, to):
-            sems = r.wo_s.at[0, step - 1], r.wo_r.at[0, step - 1]
-            return remote(r.out_send.at[step - 1], r.out_land.at[step - 1], *sems, batch=to * 2 + core)
+        def out_copy(way):
+            sems = r.wo_s.at[0, way], r.wo_r.at[0, way]
+            to = partner_at(jnp.int32(way)) * 2 + core
+            return remote(r.out_send.at[way], r.out_land.at[way], *sems, batch=to)
 
         for step in range(chips):
-            part = mm(r.gated_pair[span(lax.rem(chip + step, chips), share), :], r.gbr_pair[...])
+            to = partner(step - 1) if step else chip
+            part = mm(r.gated_pair[span(to, share), :], r.gbr_pair[...])
             if step:
                 r.out_send[step - 1] = part.astype(BF16)
             else:
@@ -907,9 +938,9 @@
 
         def wait_plane(k, dst_of):
             for at in range(peers):
-                source = group_at(groups - 1 - at)
+                source = sibling if at == 6 else partner(at // 2) * 2 + at % 2
                 dst = dst_of(source)
-                plane_copy(k, dst, dst, at, source).wait_recv()
+                remote(dst, dst, r.pa_s.at[k, at], r.pa_r.at[k, at], batch=source).wait_recv()
 
         deep = groups // 2 * tokens
 
@@ -979,7 +1010,7 @@
         tiles(tokens, length, grad_spec)
         to_tokens(3, r.gconv_c)
         for at in range(peers):
-            send("ffn", pre_copy(at, group_at(1 + at)))
+            send("ffn", pre_copy(at))
 
         def proj_back(first):
             rows = pl.ds(first, tokens + spare)
@@ -1017,18 +1048,20 @@
         in_pair.wait_recv()
         drain("in_pair")
 
-        def in_copy(step, to):
-            sems = r.wi_s.at[step - 1], r.wi_r.at[step - 1]
-            return remote(r.in_send.at[step - 1], r.in_land.at[step - 1], *sems, batch=to * 2 + core)
-
-        for step in list(range(1, chips)) + [0]:
-            to = lax.rem(chip + step, chips)
+        def in_copy(way):
+            sems = r.wi_s.at[way], r.wi_r.at[way]
+            to = partner_at(jnp.int32(way)) * 2 + core
+            return remote(r.in_send.at[way], r.in_land.at[way], *sems, batch=to)
+
+        for step in range(chips):
+            way = way_of(step) if step < chips - 1 else None
+            to = chip if way is None else partner_at(jnp.int32(way))
             part = in_part(to * 2 + core) + r.in_pair[to].astype(F32)
-            if step:
-                r.in_send[step - 1] = part.astype(BF16)
-                send("in", in_copy(step, to))
+            if way is None:
+                r.in_own[...] = part
             else:
-                r.in_own[...] = part
+                r.in_send[way] = part.astype(BF16)
+                send("in", in_copy(way))
 
         r.w12[...] = jnp.zeros((net_rows, 128), F32)
         r.sum_w3[...] = jnp.zeros((filt, own), F32)
@@ -1143,8 +1176,8 @@
                 remote(dst, dst, r.tr_s.at[k, at], r.tr_r.at[k, at], batch=source).wait_recv()
             copy.wait()
 
-        for step in range(1, chips):
-            send("out", out_copy(step, lax.rem(chip + step, chips)))
+        for step in range(chips - 1):
+            send("out", out_copy(way_of(step)))
         small_z_wait(0, lambda step: r.w12_z.at[step - 1])
         net = r.w12[...]
         for step in range(zpeers):
@@ -1178,8 +1211,8 @@
         wait_plane(1, lambda at: r.pre_own.at[span(at, tokens)])
         reduce_send(1, up_refs, turned_part(r.pre_own))
         win_loads = [(block, load_win(block)) for block in range(3)]
-        for step in range(1, chips):
-            in_copy(step, lax.rem(chip + step, chips)).wait_recv()
+        for way in range(chips - 1):
+            in_copy(way).wait_recv()
         total = r.in_own[...]
         for step in range(chips - 1):
             total = total + r.in_land[step].astype(F32)
@@ -1228,8 +1261,8 @@
         store_tokens = load(r.local_sem.at[13], r.res, r.tokens_grad)
         reduce_finish(0, down_refs)
         store_down = load(r.local_sem.at[9], down_refs[4], r.grad_w_down)
-        for step in range(1, chips):
-            out_copy(step, lax.rem(chip + step, chips)).wait_recv()
+        for way in range(chips - 1):
+            out_copy(way).wait_recv()
         total = r.xhat2[share : 2 * share, :]
         for step in range(chips - 1):
             total = total + r.out_land[step].astype(F32)

time: 204 us -> 205 us (level)
  no operation moved by 1% of the time
where the time goes in v3:
time: 205 us; the launch traced here: 204 us
  Pallas kernels  203 us (99%)
    pallas_call x1, Pallas kernels, call(): pl.pallas_call(kernel, out_shape=[jax.ShapeDtypeStruct(shape, dtype) for...  199 us
    pallas_call x1, Pallas kernels, settled(): pl.pallas_call(copy_all, out_shape=[jax.ShapeDtypeStruct(value.shape[1:]...  4.44 us

profile of v3, /device:TPU:1, one launch (start us, length us, event | category | flops | bytes accessed | tf_op | source)
XLA Modules:
  0.0 204.3 jit_solution(11972199287484865054)
XLA Ops:
  0.7 199.0 %shard_map.273 = (bf16[256,1024]{1,0:T(8,128)(2,1)}, f32[256,1024]{1,0:T(8,128)}, f32[32,3072]{1,0:T(8,128)}, f32[32,1024]{1,0:T(8,128)}, f32[32,4096]{1,0:T(8,1...) custom-call(bf16[256,1024]{1,0:T(8,128)(2,1)} %bitcast.9, ...), custom_call_target="tpu_custom_call" | custom-call | tf_op jit(solution)/shard_map/pallas_call | solution.py:1336
  199.6 4.4 %shard_map.274 = (bf16[256,1024]{1,0:T(8,128)(2,1)}, f32[256,1024]{1,0:T(8,128)}, f32[32,3072]{1,0:T(8,128)}, f32[32,1024]{1,0:T(8,128)}, f32[32,4096]{1,0:T(8,1...) custom-call(bf16[256,1024]{1,0:T(8,128)(2,1)} %get-tuple-element.39., ...), custom_call_target="tpu_custom_call" | custom-call | tf_op jit(solution)/shard_map/pallas_call | solution.py:1380

commit v4 on v3

--- a/solution.py
+++ b/solution.py
@@ -280,6 +280,7 @@
 
 MESH = pl.DeviceIdType.MESH
 KERNEL_VMEM = 63 * 1024 * 1024
+PART_BYTES = 96 * 1024
 
 
 def symmetric_tables(length):
@@ -308,6 +309,47 @@
     sin_sign = jnp.where(quarter >= 2.0, -1.0, 1.0)
     cos_sign = jnp.where((quarter == 1.0) | (quarter == 2.0), -1.0, 1.0)
     return sin_sign * jnp.where(odd, cosine, sine), cos_sign * jnp.where(odd, sine, cosine)
+
+
+class InParts:
+    def __init__(self, src, dst, send_sem, recv_sem, where):
+        self.refs, self.sems, self.where = (src, dst), (send_sem, recv_sem), where
+
+    def whole(self):
+        return self.part(*self.refs)
+
+    def part(self, src, dst):
+        return pltpu.make_async_remote_copy(
+            src_ref=src,
+            dst_ref=dst,
+            send_sem=self.sems[0],
+            recv_sem=self.sems[1],
+            device_id=self.where,
+            device_id_type=MESH,
+        )
+
+    def start(self):
+        src, dst = self.refs
+        shape, size = src.shape, math.prod(src.shape) * jnp.dtype(src.dtype).itemsize
+        want = max(1, min(8, size // PART_BYTES))
+        lead = shape[0] if len(shape) == 3 else 1
+        outer = max(count for count in range(1, lead + 1) if lead % count == 0 and count <= want)
+        inner = 1
+        while outer * inner * 2 <= want and shape[-2] % (inner * 2 * 16) == 0:
+            inner *= 2
+        rows = shape[-2] // inner
+        for first in range(outer):
+            for second in range(inner):
+                at = (pl.ds(second * rows, rows),)
+                if len(shape) == 3:
+                    at = (pl.ds(first * (lead // outer), lead // outer), *at)
+                self.part(src.at[at], dst.at[at]).start()
+
+    def wait_send(self):
+        self.whole().wait_send()
+
+    def wait_recv(self):
+        self.whole().wait_recv()
 
 
 class Named:
@@ -468,10 +510,7 @@
             return pl.ds(pl.multiple_of(at * size, size), size)
 
         def remote(src, dst, send_sem, recv_sem, **where):
-            return pltpu.make_async_remote_copy(
-                src_ref=src, dst_ref=dst, send_sem=send_sem, recv_sem=recv_sem,
-                device_id=where, device_id_type=MESH,
-            )
+            return InParts(src, dst, send_sem, recv_sem, where)
 
         def send(key, copy):
             copy.start()

time: 205 us -> 205 us (level)
  no operation moved by 1% of the time
where the time goes in v4:
time: 205 us; the launch traced here: 204 us
  Pallas kernels  203 us (99%)
    pallas_call x1, Pallas kernels, call(): pl.pallas_call(kernel, out_shape=[jax.ShapeDtypeStruct(shape, dtype) for...  199 us
    pallas_call x1, Pallas kernels, settled(): pl.pallas_call(copy_all, out_shape=[jax.ShapeDtypeStruct(value.shape[1:]...  4.44 us

profile of v4, /device:TPU:1, one launch (start us, length us, event | category | flops | bytes accessed | tf_op | source)
XLA Modules:
  0.0 204.3 jit_solution(4662512303699852050)
XLA Ops:
  0.7 199.0 %shard_map.273 = (bf16[256,1024]{1,0:T(8,128)(2,1)}, f32[256,1024]{1,0:T(8,128)}, f32[32,3072]{1,0:T(8,128)}, f32[32,1024]{1,0:T(8,128)}, f32[32,4096]{1,0:T(8,1...) custom-call(bf16[256,1024]{1,0:T(8,128)(2,1)} %bitcast.9, ...), custom_call_target="tpu_custom_call" | custom-call | tf_op jit(solution)/shard_map/pallas_call | solution.py:1375
  199.7 4.4 %shard_map.274 = (bf16[256,1024]{1,0:T(8,128)(2,1)}, f32[256,1024]{1,0:T(8,128)}, f32[32,3072]{1,0:T(8,128)}, f32[32,1024]{1,0:T(8,128)}, f32[32,4096]{1,0:T(8,1...) custom-call(bf16[256,1024]{1,0:T(8,128)(2,1)} %get-tuple-element.39., ...), custom_call_target="tpu_custom_call" | custom-call | tf_op jit(solution)/shard_map/pallas_call | solution.py:1419

commit v5 on v3

--- a/solution.py
+++ b/solution.py
@@ -327,8 +327,7 @@
     spare = 16
     chips = groups // 2
     down_rows = ffc // blocks
-    net_at = -(-emb // 8) * 8
-    net_rows = net_at + filt
+    net_rows = filt
     peers, zpeers = groups - 1, blocks - 1
     vm, hbm = pltpu.VMEM, pl.ANY
     inputs = dict(
@@ -351,8 +350,8 @@
         grad_w1=((emb, filt), F32, vm),
         grad_w2=((filt, filt), F32, vm),
         grad_w3=((filt, rows_out), F32, vm),
-        cot_land=((2, groups // 2 * tokens, width), BF16, hbm),
-        n2_land=((groups, width, tokens), BF16, hbm),
+        cot_land=((4 * tokens, width), BF16, hbm),
+        n2_land=((4, width, tokens), BF16, hbm),
     )
     dma = pltpu.SemaphoreType.DMA
     scratch = dict(
@@ -364,7 +363,7 @@
         ghalo=vm((8, 3 * width), F32), ghalo_in=vm((8, 3 * width), F32), tail=vm((16, 3 * width), F32),
         ext_c=vm((length + 32, 3 * own), BF16), gproj_c=vm((length, 3 * own), BF16),
         gconv_c=vm((length + 16, own), BF16), glong_c=vm((length + 16, own), BF16),
-        ggb=vm((tokens, width), BF16),
+
         win=vm((3, width, width), BF16), wout=vm((width, width), BF16),
         cs=vm((length, length), BF16), sn=vm((length, length), BF16),
         ext=vm((tokens + 16, 3 * width), BF16),
@@ -383,8 +382,8 @@
         w12_sum=vm((net_rows, 128), F32), w12_plane=vm((peers, net_rows, 128), F32),
         sum_w3=vm((filt, own), F32), w3_land=vm((peers, filt // groups, own), F32),
         w3_part=vm((filt // groups, own), F32), w3_all=vm((blocks, filt, own), F32),
-        hre=vm((length, own), F32), him=vm((length, own), F32),
-        xre=vm((length, own), F32), xim=vm((length, own), F32),
+        hre=vm((length, own), BF16), him=vm((length, own), BF16),
+        xre=vm((length, own), BF16), xim=vm((length, own), BF16),
         yre=vm((length, own), BF16), yim=vm((length, own), BF16),
         qre=vm((length, own), BF16), qim=vm((length, own), BF16),
         conv_out=vm((length + 16, own), BF16), conv_in=vm((blocks, tokens, own), BF16),
@@ -392,15 +391,15 @@
         res=vm((tokens, width), F32), xhat2=vm((tokens, width), F32),
         inv2=vm((tokens, 128), F32), gn2=vm((tokens, width), F32),
         gres=vm((tokens, width), F32),
-        hid_send=vm((groups, ffc, tokens), BF16), hid_own=vm((ffc, groups * tokens), BF16),
-        pre_send=vm((groups, tokens, ffc), BF16), pre_own=vm((groups * tokens, ffc), BF16),
+        hid_send=vm((groups, ffc, tokens), BF16), hid_own=vm((2, ffc, 4 * tokens), BF16),
+        pre_send=vm((groups, tokens, ffc), BF16), pre_own=vm((2, 4 * tokens, ffc), BF16),
         gbr_pair=vm((2 * tokens, width), BF16),
         glong=vm((tokens, width), BF16),
         gproj=vm((tokens, 3 * width), BF16),
-        down_send=vm((2, down_rows, width), BF16), down_land=vm((2, down_rows, width), BF16),
-        down_next=vm((down_rows, width), BF16), down_last=vm((down_rows, width), BF16),
-        up_send=vm((2, own, ffc), BF16), up_land=vm((2, own, ffc), BF16),
-        up_next=vm((own, ffc), BF16), up_last=vm((own, ffc), BF16),
+        down_send=vm((4, down_rows, width), BF16), down_first=vm((4, down_rows, width), BF16),
+        down_land=vm((2, down_rows, width), BF16), down_last=vm((down_rows, width), BF16),
+        up_send=vm((4, own, ffc), BF16), up_first=vm((4, own, ffc), BF16),
+        up_land=vm((2, own, ffc), BF16), up_last=vm((own, ffc), BF16),
         in_send=vm((chips, share, 3 * own), BF16), in_pair=vm((chips, share, 3 * own), BF16),
         in_land=vm((chips - 1, share, 3 * own), BF16), in_own=vm((share, 3 * own), F32),
         out_send=vm((chips - 1, share, width), BF16), out_land=vm((chips - 1, share, width), BF16),
@@ -411,11 +410,11 @@
         win_sem=dma((3,)),
         ffn_sem=dma((2, 2)),
         local_sem=dma((16,)),
-        stage_sem=dma((chips - 1,)),
-        ag_s=dma((2, groups - 1)), ag_r=dma((2, groups - 1)),
+        stage_sem=dma((2,)),
+        ag_s=dma((2, 3)), ag_r=dma((2, 3)), fs_s=dma((2,)), fs_r=dma((2,)),
         halo_s=dma((2,)), halo_r=dma((2,)),
         za_s=dma((4, zpeers)), za_r=dma((4, zpeers)),
-        pa_s=dma((2, peers)), pa_r=dma((2, peers)),
+        pa_s=dma((2, 6)), pa_r=dma((2, 6)),
         cx_s=dma((3,)), cx_r=dma((3,)), zg_s=dma((zpeers,)), zg_r=dma((zpeers,)),
         wi_s=dma((chips - 1,)), wi_r=dma((chips - 1,)), ti_s=dma((zpeers, 3)), ti_r=dma((zpeers, 3)), wo_s=dma((2, chips - 1)), wo_r=dma((2, chips - 1)),
         rs_s=dma((2, 2)), rs_r=dma((2, 2)),
@@ -448,15 +447,16 @@
         def partner_at(way):
             return flipped(1 - lax.rem(way, 2), lax.div(way + 1, 2))
 
-        def peer(at):
-            at = jnp.int32(at)
-            late, last = lax.div(at, 4), lax.div(at, 6)
-            way = (1 - late) * lax.rem(at + core, 2) + late * 2
-            to_core = (1 - late) * lax.div(at, 2) + late * (at - 4)
-            to_chip = flipped((1 - last) * (1 - lax.rem(way, 2)), (1 - last) * lax.div(way + 1, 2))
-            own_chip = (7 - at) * (1 - core) + (at - 6) * core
-            group = to_chip * 2 + (1 - last) * to_core + last * own_chip
-            return group, (1 - last) * (way * 2 + to_core) + last * 6, (1 - last) * (way * 2 + core) + last * 6
+        def flip(value, turn):
+            return value + turn - 2 * value * turn
+
+        def turns(at):
+            rest = 7 - at
+            return lax.rem(rest, 2), lax.rem(lax.div(rest, 2), 2), lax.div(rest, 4)
+
+        def chunk_group(at):
+            turn_core, turn_x, turn_y = turns(jnp.int32(at))
+            return (flip(chip_y, turn_y) * 2 + flip(chip_x, turn_x)) * 2 + flip(core, turn_core)
 
         def group_at(step):
             return lax.rem(b + step, groups)
@@ -511,45 +511,37 @@
         for step in range(1, blocks):
             pl.semaphore_signal(barrier, inc=1, device_id={"seq": block_at(step)}, device_id_type=MESH)
 
-        slots = [
-            lambda at: r.cot_land.at[lax.div(at, chips), span(lax.rem(at, chips), tokens)],
-            lambda at: r.n2_land.at[at],
-        ]
-
-        def gather_copy(k, at, src, slot, to):
-            return remote(src, slot, r.ag_s.at[k, at], r.ag_r.at[k, at], batch=to)
+        def member(k, turn_side, turn_core):
+            side = chip_y if k else chip_x
+            return flip(side, turn_side) * 2 + flip(core, turn_core)
+
+        def slot(k, at):
+            return r.n2_land.at[at] if k else r.cot_land.at[span(at, tokens)]
+
+        def gather_copy(k, at, src, dst, to):
+            return remote(src, dst, r.ag_s.at[k, at], r.ag_r.at[k, at], batch=to)
 
         def gather_local(k, src):
-            return pltpu.make_async_copy(src, slots[k](b), r.local_sem.at[k])
+            return pltpu.make_async_copy(src, slot(k, member(k, 0, 0)), r.local_sem.at[k])
 
         def gather_start(k, src):
-            for step in range(chips - 1):
-                way = way_of(step)
-                to = partner_at(jnp.int32(way)) * 2 + core
-                send(("ag", k), gather_copy(k, way, src, slots[k](b), to))
-            send(("ag", k), gather_copy(k, chips - 1, src, slots[k](b), sibling))
+            dst = slot(k, member(k, 0, 0))
+            send(("ag", k), gather_copy(k, 0, src, dst, partner(k) * 2 + core))
+            send(("ag", k), gather_copy(k, 1, src, dst, sibling))
             gather_local(k, src).start(priority=1)
 
-        def stage(k, step):
-            if k == 0:
-                return r.gproj.at[:, (step - 1) * width : step * width]
-            return r.win.at[0, :, (step - 1) * tokens : step * tokens]
-
         def gather_forward(k):
-            staged = []
-            for step in range(1, chips):
-                slot = slots[k](partner(step - 1) * 2 + core)
-                gather_copy(k, step - 1, slot, slot, sibling).wait_recv()
-                staged.append((slot, load(r.stage_sem.at[step - 1], slot, stage(k, step))))
-            for step, (slot, copy) in enumerate(staged, 1):
-                copy.wait()
-                source = stage(k, step)
-                send(("forward", k), gather_copy(k, chips - 1 + step, source, slot, sibling))
-
-        def gather_finish(k):
-            for step in range(chips):
-                slot = slots[k]((partner(step - 1) if step else chip) * 2 + 1 - core)
-                gather_copy(k, chips - 1 + step, slot, slot, sibling).wait_recv()
+            dst = slot(k, member(k, 1, 0))
+            gather_copy(k, 0, dst, dst, sibling).wait_recv()
+            staged = r.win.at[2, :, 3 * own : 3 * own + tokens] if k else r.gproj.at[:, 0:width]
+            load(r.stage_sem.at[k], dst, staged).wait()
+            send(("forward", k), gather_copy(k, 2, staged, dst, sibling))
+
+        def gather_finish(k, src):
+            gather_local(k, src).wait()
+            for at in range(2):
+                dst = slot(k, member(k, at, 1))
+                gather_copy(k, 1 + at, dst, dst, sibling).wait_recv()
 
         def turned(value_ref, out_ref):
             def body(at):
@@ -604,13 +596,13 @@
         r.ext_c[length + spare :, :] = jnp.zeros((spare, 3 * own), BF16)
 
         def up_weights(at, slot):
-            group = peer(at)[0]
+            group = chunk_group(at)
             return pltpu.make_async_copy(
                 r.w_up.at[:, span(group, ffc)], r.win.at[0, :, span(slot, ffc)], r.ffn_sem.at[slot, 0]
             )
 
         def down_weights(at, slot):
-            group = peer(at)[0]
+            group = chunk_group(at)
             return pltpu.make_async_copy(
                 r.w_down.at[span(group, ffc)], r.win.at[1, span(slot, ffc)], r.ffn_sem.at[slot, 1]
             )
@@ -690,8 +682,8 @@
             real = mm(r.cs[rows, :], r.qre[...]) * scale
             imag = mm(r.sn[rows, :], r.qre[...]) * -scale
             turn_re, turn_im = r.phase[rows, 0:1], r.phase[rows, 1:2]
-            r.hre[rows, :] = real * turn_re - imag * turn_im
-            r.him[rows, :] = real * turn_im + imag * turn_re
+            r.hre[rows, :] = (real * turn_re - imag * turn_im).astype(BF16)
+            r.him[rows, :] = (real * turn_im + imag * turn_re).astype(BF16)
 
         tiles(tokens, length, taps_spec)
 
@@ -701,9 +693,9 @@
             rows = pl.ds(at, tokens)
             real = mm(r.cs[rows, :], r.chan[0:length, :])
             imag = -mm(r.sn[rows, :], r.chan[0:length, :])
-            r.xre[rows, :] = real
-            r.xim[rows, :] = imag
-            hre, him = r.hre[rows, :], r.him[rows, :]
+            r.xre[rows, :] = real.astype(BF16)
+            r.xim[rows, :] = imag.astype(BF16)
+            hre, him = r.hre[rows, :].astype(F32), r.him[rows, :].astype(F32)
             r.yre[rows, :] = (hre * real - him * imag).astype(BF16)
             r.yim[rows, :] = (-(hre * imag + him * real)).astype(BF16)
 
@@ -790,17 +782,24 @@
 
         tiles(32, tokens, norm2)
         turned(r.half, r.turn)
+        gather_start(1, r.turn)
         r.gn2[...] = jnp.zeros((tokens, width), F32)
 
-        def plane_copy(k, src, dst, at):
-            to, send_at, recv_at = peer(at)
-            return remote(src, dst, r.pa_s.at[k, send_at], r.pa_r.at[k, recv_at], batch=to)
-
-        def hidden_copy(at):
-            return plane_copy(0, r.hid_send.at[at], r.hid_own.at[:, span(b, tokens)], at)
-
-        def pre_copy(at):
-            return plane_copy(1, r.pre_send.at[at], r.pre_own.at[span(b, tokens)], at)
+        def plane_copy(k, at):
+            turn_core, turn_x, turn_y = turns(jnp.int32(at))
+            turn_side, turn_far = (turn_y, turn_x) if k else (turn_x, turn_y)
+            index = turn_far * 3 + turn_side * 2 + turn_core - 1
+            if k:
+                to = (flip(chip_y, turn_y) * 2 + chip_x) * 2 + flip(core, turn_core)
+                src, dst = r.pre_send.at[at], r.pre_own.at[flip(chip_x, turn_x), span(member(1, 0, 0), tokens)]
+            else:
+                to = (chip_y * 2 + flip(chip_x, turn_x)) * 2 + flip(core, turn_core)
+                src = r.hid_send.at[at]
+                dst = r.hid_own.at[flip(chip_y, turn_y), :, span(member(0, 0, 0), tokens)]
+            return remote(src, dst, r.pa_s.at[k, index], r.pa_r.at[k, index], batch=to)
+
+        hidden_remote = [0, 1, 2, 4, 5, 6]
+        pre_remote = [0, 1, 2, 3, 4, 6]
 
         def chunk(at, carry):
             slot = lax.rem(at, 2)
@@ -823,9 +822,13 @@
             tiles(32, tokens, act)
             r.hid_send[at] = r.hid_buf[...].T
 
-            @pl.when(at < groups - 1)
+            @pl.when(lax.rem(at, 4) < 3)
             def _():
-                hidden_copy(at).start()
+                plane_copy(0, at).start()
+
+            @pl.when((at < 5) | (at == 6))
+            def _():
+                plane_copy(1, at).start()
 
             down_weights(at, slot).wait()
             r.res[...] += mm(r.hid_buf[...], r.win[1, where, :])
@@ -839,25 +842,15 @@
             return carry
 
         lax.fori_loop(0, groups, chunk, 0)
-        for at in range(peers):
-            sent.setdefault("ffn", []).append(hidden_copy(at))
-
-        def pool_cot():
-            return [load(r.win_sem.at[half], r.cot_land.at[half], r.win.at[half]) for half in range(2)]
-
-        def pool_turned(land):
-            return [
-                load(
-                    r.pool_sem.at[at],
-                    land.at[at],
-                    r.win.at[at // chips, :, pl.ds(at % chips * tokens, tokens)],
-                )
-                for at in range(groups)
-            ]
-
-        gather_forward(0)
-        r.hid_own[:, span(b, tokens)] = r.hid_send[groups - 1]
-        r.pre_own[span(b, tokens), :] = r.pre_send[groups - 1]
+        for at in hidden_remote:
+            sent.setdefault("ffn", []).append(plane_copy(0, at))
+        for at in pre_remote:
+            sent.setdefault("ffn", []).append(plane_copy(1, at))
+
+        for turn, at in ((0, 7), (1, 3)):
+            r.hid_own[flip(chip_y, turn), :, span(member(0, 0, 0), tokens)] = r.hid_send[at]
+        for turn, at in ((0, 7), (1, 5)):
+            r.pre_own[flip(chip_x, turn), span(member(1, 0, 0), tokens), :] = r.pre_send[at]
 
         def norm2_back(at, total):
             rows = pl.ds(pl.multiple_of(at * 32, 32), 32)
@@ -879,15 +872,16 @@
             grad = mm_nt(r.gbr_pair[mine, :], r.wout[span(block, own), :])
             glong = (grad * r.gate_out[:, cols]).astype(BF16)
             r.glong[:, cols] = glong
-            r.ggb[:, cols] = grad.astype(BF16)
+            r.tok[:, cols] = grad.astype(BF16)
             r.long[:, cols] = grad * r.long[:, cols]
             r.sum_bias[:, cols] = jnp.sum(
                 glong.astype(F32) * r.sig[:, cols].astype(F32), axis=0, keepdims=True
             )
 
-        to_channels(2, r.ggb, gated_back)
-
-        gather_start(1, r.turn)
+        to_channels(2, r.tok, gated_back)
+        gather_forward(0)
+        gather_forward(1)
+
 
         branch_copy.wait_recv()
         gated_copy.wait_recv()
@@ -908,57 +902,73 @@
         near = z + 1 - 2 * lax.rem(z, 2)
         far = block_at(2)
 
+        def reduce_zero_copy(k, refs):
+            to = partner(0 if k else 1) * 2 + core
+            return remote(refs[0], refs[1], r.fs_s.at[k], r.fs_r.at[k], batch=to)
+
         def reduce_first(k, refs):
-            return remote(refs[0], refs[1], r.rs_s.at[k, 0], r.rs_r.at[k, 0], seq=near)
+            return remote(refs[0].at[0:2], refs[2], r.rs_s.at[k, 0], r.rs_r.at[k, 0], seq=near)
 
         def reduce_second(k, refs):
-            return remote(refs[2], refs[3], r.rs_s.at[k, 1], r.rs_r.at[k, 1], seq=far)
+            return remote(refs[0].at[2], refs[3], r.rs_s.at[k, 1], r.rs_r.at[k, 1], seq=far)
+
+        def reduce_zero(k, refs, part_of):
+            other = 1 - (chip_x if k else chip_y)
+            for block in range(blocks):
+                refs[0][block] = part_of(other, block).astype(BF16)
+            send(("zero", k), reduce_zero_copy(k, refs))
 
         def reduce_send(k, refs, part_of):
-            send_ref, _, next_ref, _, own_ref = refs
-            send_ref[0] = part_of(near).astype(BF16)
-            send_ref[1] = part_of(lax.rem(near + 2, blocks)).astype(BF16)
+            reduce_zero_copy(k, refs).wait_recv()
+            drain(("zero", k))
+            mine_too = chip_x if k else chip_y
+
+            def total(block):
+                return part_of(mine_too, block) + refs[1][block].astype(F32)
+
+            refs[0][0] = total(near).astype(BF16)
+            refs[0][1] = total(lax.rem(near + 2, blocks)).astype(BF16)
             send("rs", reduce_first(k, refs))
-            next_ref[...] = part_of(far).astype(BF16)
-            own_ref[...] = part_of(z)
+            refs[0][2] = total(far).astype(BF16)
+            refs[4][...] = total(z)
 
         def reduce_next(k, refs):
-            _, land_ref, next_ref, _, own_ref = refs
             reduce_first(k, refs).wait_recv()
-            next_ref[...] = (next_ref[...].astype(F32) + land_ref[1].astype(F32)).astype(BF16)
+            refs[0][2] = (refs[0][2].astype(F32) + refs[2][1].astype(F32)).astype(BF16)
             send("rs", reduce_second(k, refs))
-            own_ref[...] += land_ref[0].astype(F32)
+            refs[4][...] += refs[2][0].astype(F32)
 
         def reduce_finish(k, refs):
             reduce_second(k, refs).wait_recv()
             refs[4][...] += refs[3][...].astype(F32)
 
-        down_refs = (r.down_send, r.down_land, r.down_next, r.down_last, r.xhat2.at[0:down_rows])
-        up_refs = (r.up_send, r.up_land, r.up_next, r.up_last, r.gate_out.at[:, 0:ffc])
-
-        def wait_plane(k, dst_of):
-            for at in range(peers):
-                source = sibling if at == 6 else partner(at // 2) * 2 + at % 2
-                dst = dst_of(source)
-                remote(dst, dst, r.pa_s.at[k, at], r.pa_r.at[k, at], batch=source).wait_recv()
-
-        deep = groups // 2 * tokens
-
-        def down_part(block):
-            rows = span(block, ffc // blocks)
-            return mm(r.hid_own[rows, :deep], r.win[0]) + mm(r.hid_own[rows, deep:], r.win[1])
-
-        def turned_part(right_ref):
-            def part(block):
-                rows = span(block, own)
-                return mm(r.win[0, rows, :], right_ref[:deep]) + mm(r.win[1, rows, :], right_ref[deep:])
-
-            return part
-
-
-        gather_local(0, r.cotv).wait()
-        gather_finish(0)
-        pool = pool_cot()
+        down_refs = (r.down_send, r.down_first, r.down_land, r.down_last, r.xhat2.at[0:down_rows])
+        up_refs = (r.up_send, r.up_first, r.up_land, r.up_last, r.gate_out.at[:, 0:ffc])
+
+        def wait_plane(k):
+            for at in pre_remote if k else hidden_remote:
+                plane_copy(k, at).wait_recv()
+
+        def down_part(group, block):
+            return mm(r.hid_own[group, span(block, down_rows), :], r.win[0])
+
+        def up_part(group, block):
+            return mm(r.win[1, span(block, own), :], r.pre_own[group])
+
+        gather_finish(0, r.cotv)
+        cot_pool = load(r.pool_sem.at[4], r.cot_land, r.win.at[0])
+        gather_finish(1, r.turn)
+        pool = [
+            load(r.pool_sem.at[at], r.n2_land.at[at], r.win.at[1, :, pl.ds(at * tokens, tokens)])
+            for at in range(4)
+        ]
+        cot_pool.wait()
+        wait_plane(0)
+        reduce_zero(0, down_refs, down_part)
+        for copy in pool:
+            copy.wait()
+        wait_plane(1)
+        reduce_zero(1, up_refs, up_part)
 
         for step in range(1, blocks):
             source = block_at(blocks - step)
@@ -997,10 +1007,10 @@
             rows = pl.ds(at, tokens)
             real = mm(r.cs[rows, :], r.glong_c[0:length, :])
             imag = -mm(r.sn[rows, :], r.glong_c[0:length, :])
-            hre, him = r.hre[rows, :], r.him[rows, :]
+            hre, him = r.hre[rows, :].astype(F32), r.him[rows, :].astype(F32)
             r.yre[rows, :] = (hre * real + him * imag).astype(BF16)
             r.yim[rows, :] = (him * real - hre * imag).astype(BF16)
-            xre, xim = r.xre[rows, :], r.xim[rows, :]
+            xre, xim = r.xre[rows, :].astype(F32), r.xim[rows, :].astype(F32)
             both_re = xre * real + xim * imag
             both_im = xre * imag - xim * real
             turn_re, turn_im = r.phase[rows, 0:1], r.phase[rows, 1:2]
@@ -1009,8 +1019,6 @@
 
         tiles(tokens, length, grad_spec)
         to_tokens(3, r.gconv_c)
-        for at in range(peers):
-            send("ffn", pre_copy(at))
 
         def proj_back(first):
             rows = pl.ds(first, tokens + spare)
@@ -1041,10 +1049,6 @@
             r.in_send[at] = in_part(at * 2 + 1 - core).astype(BF16)
         in_pair = pair_copy(2, r.in_send, r.in_pair)
         send("in_pair", in_pair)
-        for copy in pool:
-            copy.wait()
-        wait_plane(0, lambda at: r.hid_own.at[:, span(at, tokens)])
-        reduce_send(0, down_refs, down_part)
         in_pair.wait_recv()
         drain("in_pair")
 
@@ -1071,9 +1075,9 @@
             grad_filt = grad_taps * fading(at)
             r.sum_w3[...] += mm(r.h2[:, rows], grad_filt, precision=HIGHEST)
             grad_angle2 = mm_nt(r.w3[...], grad_filt, precision=HIGHEST) * r.s2[:, rows]
-            r.w12[net_at:, :filt] += mm_nt(r.h1[:, rows], grad_angle2, precision=HIGHEST)
+            r.w12[:, :filt] += mm_nt(r.h1[:, rows], grad_angle2, precision=HIGHEST)
             grad_angle1 = mm(r.filt_w2[...], grad_angle2, precision=HIGHEST) * r.s1[:, rows]
-            r.w12[:emb, :filt] += mm_nt(r.features_t[:, rows], grad_angle1, precision=HIGHEST)
+            r.w12[:emb, filt : 2 * filt] += mm_nt(r.features_t[:, rows], grad_angle1, precision=HIGHEST)
 
         def small_copy(k, src, dst, at, to):
             return remote(src, dst, r.sm_s.at[k, at], r.sm_r.at[k, at], batch=to)
@@ -1103,6 +1107,11 @@
         w3_rows = filt // groups
         small_z_send(0, r.w12, lambda step: r.w12_z.at[step - 1])
         small_send(0, lambda to: r.sum_w3.at[span(to, w3_rows)], lambda at: r.w3_land.at[at])
+
+        reduce_send(0, down_refs, down_part)
+        reduce_send(1, up_refs, up_part)
+        drain(("forward", 1))
+        win_loads = [(block, load_win(block)) for block in range(3)]
 
         def outz_copy(step, to):
             sems = r.wo_s.at[1, step - 1], r.wo_r.at[1, step - 1]
@@ -1146,7 +1155,6 @@
         tiles(128, width, mixed_cols)
         halo = remote(r.ghalo, r.ghalo_in, r.halo_s.at[1], r.halo_r.at[1], seq=block_at(blocks - 1))
         send("halo", halo)
-        gather_forward(1)
         halo.wait_recv()
         later = r.ghalo_in[...] * jnp.where(z < blocks - 1, 1.0, 0.0)
 
@@ -1192,25 +1200,16 @@
         r.w3_all[z, span(b, w3_rows), :] = part
         small_send(2, lambda to: r.w3_part, lambda at: r.w3_all.at[z, span(b, w3_rows)])
         reduce_next(0, down_refs)
-        gather_local(1, r.turn).wait()
-        gather_finish(1)
-        drain(("forward", 1))
-        pool = pool_turned(r.n2_land)
         small_wait(1, lambda at: r.w12_plane.at[at])
         net = r.w12_sum[...]
         for at in range(peers):
             net = net + r.w12_plane[at]
-        r.grad_w1[...] = net[:emb, :filt]
-        r.grad_w2[...] = net[net_at:, :filt]
+        r.grad_w1[...] = net[:emb, filt : 2 * filt]
+        r.grad_w2[...] = net[:, :filt]
         for at in range(peers):
             dst = r.w3_all.at[z, span(group_at(groups - 1 - at), w3_rows)]
             small_copy(2, dst, dst, at, group_at(groups - 1 - at)).wait_recv()
         small_z_send(1, r.w3_all.at[z], lambda step: r.w3_all.at[z])
-        for copy in pool:
-            copy.wait()
-        wait_plane(1, lambda at: r.pre_own.at[span(at, tokens)])
-        reduce_send(1, up_refs, turned_part(r.pre_own))
-        win_loads = [(block, load_win(block)) for block in range(3)]
         for way in range(chips - 1):
             in_copy(way).wait_recv()
         total = r.in_own[...]
@@ -1236,6 +1235,9 @@
         r.gn2[...] += mm_nt(r.gproj[:, 2 * width :], r.win[2])
 
         reduce_next(1, up_refs)
+        drain(("za", 2))
+        load(r.load_sem.at[0], r.tokens, r.tok).wait()
+
         def norm1_back(at, total):
             rows = pl.ds(pl.multiple_of(at * 32, 32), 32)
             grad, inverse = r.gn2[rows, :], r.inv1[rows, 0:1]

time: 205 us -> 207 us (level)
  Pallas kernels: 203 us -> 206 us
    pallas_call x1, Pallas kernels: 199 us -> 201 us  [call(): pl.pallas_call(kernel, out_shape=[jax.ShapeDtypeStruct(shape, dtype) for...]
where the time goes in v5:
time: 207 us
  Pallas kernels  206 us (100%)
    pallas_call x1, Pallas kernels, call(): pl.pallas_call(kernel, out_shape=[jax.ShapeDtypeStruct(shape, dtype) for...  201 us
    pallas_call x1, Pallas kernels, settled(): pl.pallas_call(copy_all, out_shape=[jax.ShapeDtypeStruct(value.shape[1:]...  4.44 us

profile of v5, /device:TPU:1, one launch (start us, length us, event | category | flops | bytes accessed | tf_op | source)
XLA Modules:
  0.0 206.8 jit_solution(17467840883183768511)
XLA Ops:
  0.7 201.5 %shard_map.273 = (bf16[256,1024]{1,0:T(8,128)(2,1)}, f32[256,1024]{1,0:T(8,128)}, f32[32,3072]{1,0:T(8,128)}, f32[32,1024]{1,0:T(8,128)}, f32[32,4096]{1,0:T(8,1...) custom-call(bf16[256,1024]{1,0:T(8,128)(2,1)} %bitcast.9, ...), custom_call_target="tpu_custom_call" | custom-call | tf_op jit(solution)/shard_map/pallas_call | solution.py:1338
  202.1 4.4 %shard_map.274 = (bf16[256,1024]{1,0:T(8,128)(2,1)}, f32[256,1024]{1,0:T(8,128)}, f32[32,3072]{1,0:T(8,128)}, f32[32,1024]{1,0:T(8,128)}, f32[32,4096]{1,0:T(8,1...) custom-call(bf16[256,1024]{1,0:T(8,128)(2,1)} %get-tuple-element.39., ...), custom_call_target="tpu_custom_call" | custom-call | tf_op jit(solution)/shard_map/pallas_call | solution.py:1382

commit v6 on v5

--- a/solution.py
+++ b/solution.py
@@ -381,7 +381,7 @@
         w12=vm((net_rows, 128), F32), w12_z=vm((zpeers, net_rows, 128), F32),
         w12_sum=vm((net_rows, 128), F32), w12_plane=vm((peers, net_rows, 128), F32),
         sum_w3=vm((filt, own), F32), w3_land=vm((peers, filt // groups, own), F32),
-        w3_part=vm((filt // groups, own), F32), w3_all=vm((blocks, filt, own), F32),
+        w3_part=vm((filt // groups, own), F32), w3_all=vm((filt, own), F32), w3_half=vm((filt, share), F32),
         hre=vm((length, own), BF16), him=vm((length, own), BF16),
         xre=vm((length, own), BF16), xim=vm((length, own), BF16),
         yre=vm((length, own), BF16), yim=vm((length, own), BF16),
@@ -415,7 +415,7 @@
         halo_s=dma((2,)), halo_r=dma((2,)),
         za_s=dma((4, zpeers)), za_r=dma((4, zpeers)),
         pa_s=dma((2, 6)), pa_r=dma((2, 6)),
-        cx_s=dma((3,)), cx_r=dma((3,)), zg_s=dma((zpeers,)), zg_r=dma((zpeers,)),
+        cx_s=dma((3,)), cx_r=dma((3,)), zg_s=dma((2, zpeers)), zg_r=dma((2, zpeers)),
         wi_s=dma((chips - 1,)), wi_r=dma((chips - 1,)), ti_s=dma((zpeers, 3)), ti_r=dma((zpeers, 3)), wo_s=dma((2, chips - 1)), wo_r=dma((2, chips - 1)),
         rs_s=dma((2, 2)), rs_r=dma((2, 2)),
         sm_s=dma((4, peers)), sm_r=dma((4, peers)),
@@ -721,14 +721,32 @@
 
         to_tokens(1, r.conv_out)
 
-        def seq_gather(step, source, to):
-            rows = r.n1_all.at[span(source, tokens)]
-            return remote(rows, rows, r.zg_s.at[step - 1], r.zg_r.at[step - 1], seq=to)
-
-        for step in range(1, blocks):
-            send("n1", seq_gather(step, z, block_at(step)))
-
-        load_wout.wait()
+        def seq_copy(down, step):
+            block = lax.rem(z + step, blocks) if down else lax.rem(z + blocks - step, blocks)
+            to = block_at(blocks - 1 if down else 1)
+            rows = r.n1_all.at[span(block, tokens)]
+            return remote(rows, rows, r.zg_s.at[down, step], r.zg_r.at[down, step], seq=to)
+
+        def seq_sends(down, step):
+            return (z > 0) & (z + step < blocks) if down else (z < blocks - 1) & (z >= step)
+
+        def seq_receives(down, step):
+            return z + 1 + step < blocks if down else z >= 1 + step
+
+        def seq_step(step):
+            for down in range(2):
+                if step:
+
+                    @pl.when(seq_receives(down, step - 1))
+                    def _():
+                        seq_copy(down, step - 1).wait_recv()
+
+                if step < zpeers:
+
+                    @pl.when(seq_sends(down, step))
+                    def _():
+                        seq_copy(down, step).start()
+
         def gate_cols(at):
             cols = pl.ds(at, 128)
             r.gate_out[:, cols] = mix(cols)[1]
@@ -743,7 +761,9 @@
             return carry
 
         lax.fori_loop(0, groups, grad_hidden, 0)
+        load_wout.wait()
         wait_tokens(1)
+        seq_step(0)
 
         def conv_cols(at):
             return r.conv_in[
@@ -841,7 +861,10 @@
 
             return carry
 
-        lax.fori_loop(0, groups, chunk, 0)
+        lax.fori_loop(0, groups // 2, chunk, 0)
+        seq_step(1)
+        lax.fori_loop(groups // 2, groups, chunk, 0)
+        seq_step(2)
         for at in hidden_remote:
             sent.setdefault("ffn", []).append(plane_copy(0, at))
         for at in pre_remote:
@@ -970,9 +993,7 @@
         wait_plane(1)
         reduce_zero(1, up_refs, up_part)
 
-        for step in range(1, blocks):
-            source = block_at(blocks - step)
-            seq_gather(step, source, source).wait_recv()
+        seq_step(3)
         for copy in own_loads:
             copy.wait()
 
@@ -1197,8 +1218,8 @@
         for at in range(peers):
             part = part + r.w3_land[at]
         r.w3_part[...] = part
-        r.w3_all[z, span(b, w3_rows), :] = part
-        small_send(2, lambda to: r.w3_part, lambda at: r.w3_all.at[z, span(b, w3_rows)])
+        r.w3_all[span(b, w3_rows), :] = part
+        small_send(2, lambda to: r.w3_part, lambda at: r.w3_all.at[span(b, w3_rows)])
         reduce_next(0, down_refs)
         small_wait(1, lambda at: r.w12_plane.at[at])
         net = r.w12_sum[...]
@@ -1207,9 +1228,24 @@
         r.grad_w1[...] = net[:emb, filt : 2 * filt]
         r.grad_w2[...] = net[:, :filt]
         for at in range(peers):
-            dst = r.w3_all.at[z, span(group_at(groups - 1 - at), w3_rows)]
+            dst = r.w3_all.at[span(group_at(groups - 1 - at), w3_rows)]
             small_copy(2, dst, dst, at, group_at(groups - 1 - at)).wait_recv()
-        small_z_send(1, r.w3_all.at[z], lambda step: r.w3_all.at[z])
+        holder, halves = lax.div(b * share, own), own // share
+        third = r.w3_all[...]
+        picked = third[:, :share]
+        for half in range(1, halves):
+            here = lax.rem(b, halves) == half
+            picked = jnp.where(here, third[:, half * share : (half + 1) * share], picked)
+
+        def w3_copy(step, to):
+            return small_z_copy(1, r.w3_half, r.w3_half, step, to)
+
+        @pl.when(z == holder)
+        def _():
+            r.w3_half[...] = picked
+            for step in range(1, blocks):
+                w3_copy(step, block_at(step)).start()
+
         for way in range(chips - 1):
             in_copy(way).wait_recv()
         total = r.in_own[...]
@@ -1298,17 +1334,16 @@
                 picked = jnp.where(z == block, value[:, block * size : (block + 1) * size], picked)
             return picked
 
-        for step in range(1, blocks):
-            source = block_at(blocks - step)
-            dst = r.w3_all.at[source]
-            small_z_copy(1, dst, dst, step, source).wait_recv()
-        third = r.w3_all[lax.div(b * share, own)]
-        halves = own // share
-        picked = third[:, :share]
-        for half in range(1, halves):
-            here = lax.rem(b, halves) == half
-            picked = jnp.where(here, third[:, half * share : (half + 1) * share], picked)
-        r.grad_w3[...] = chosen(picked, rows_out)
+        @pl.when(z == holder)
+        def _():
+            for step in range(1, blocks):
+                w3_copy(step, block_at(step)).wait_send()
+
+        @pl.when(z != holder)
+        def _():
+            w3_copy(lax.rem(z + blocks - holder, blocks), holder).wait_recv()
+
+        r.grad_w3[...] = chosen(r.w3_half[...], rows_out)
         small_z_wait(2, lambda step: r.small_z.at[step - 1])
         small = r.small_sum[...]
         for step in range(zpeers):
@@ -1328,6 +1363,13 @@
                 in_spread(step, part, source, source).wait_recv()
             in_spread(0, part, z, z).wait()
         store_layer.wait()
+        for down in range(2):
+            for step in range(zpeers):
+
+                @pl.when(seq_sends(down, step))
+                def _():
+                    seq_copy(down, step).wait_send()
+
         store_down.wait()
         store_out.wait()
         store_tokens.wait()

time: 207 us -> 192 us (0.928)
  Pallas kernels: 206 us -> 191 us
    pallas_call x1, Pallas kernels: 201 us -> 187 us  [call(): pl.pallas_call(kernel, out_shape=[jax.ShapeDtypeStruct(shape, dtype) for...]
where the time goes in v6:
time: 192 us
  Pallas kernels  191 us (99%)
    pallas_call x1, Pallas kernels, call(): pl.pallas_call(kernel, out_shape=[jax.ShapeDtypeStruct(shape, dtype) for...  187 us
    pallas_call x1, Pallas kernels, settled(): pl.pallas_call(copy_all, out_shape=[jax.ShapeDtypeStruct(value.shape[1:]...  4.44 us

profile of v6, /device:TPU:1, one launch (start us, length us, event | category | flops | bytes accessed | tf_op | source)
XLA Modules:
  0.0 191.9 jit_solution(8843892692739887303)
XLA Ops:
  0.7 186.6 %shard_map.273 = (bf16[256,1024]{1,0:T(8,128)(2,1)}, f32[256,1024]{1,0:T(8,128)}, f32[32,3072]{1,0:T(8,128)}, f32[32,1024]{1,0:T(8,128)}, f32[32,4096]{1,0:T(8,1...) custom-call(bf16[256,1024]{1,0:T(8,128)(2,1)} %bitcast.9, ...), custom_call_target="tpu_custom_call" | custom-call | tf_op jit(solution)/shard_map/pallas_call | solution.py:1380
  187.3 4.4 %shard_map.274 = (bf16[256,1024]{1,0:T(8,128)(2,1)}, f32[256,1024]{1,0:T(8,128)}, f32[32,3072]{1,0:T(8,128)}, f32[32,1024]{1,0:T(8,128)}, f32[32,4096]{1,0:T(8,1...) custom-call(bf16[256,1024]{1,0:T(8,128)(2,1)} %get-tuple-element.39., ...), custom_call_target="tpu_custom_call" | custom-call | tf_op jit(solution)/shard_map/pallas_call | solution.py:1424
